TPU v7x, 32 devices: a whole 2x2x4 slice. The times are simulated.
32 devices in a mesh: groups: 2 (over x), dp: 16 (over z, y, core), tensor: 1.
Axes of the slice: x: 2, y: 2, z: 4, core: 2. Of those that a mesh axis runs over, the one named last changes fastest.
Arguments:
- doc_hidden: bfloat16 [1280, 32, 4096], P(('groups', 'dp'), None, 'tensor'), parts along dimension 0, may hold values from -6 to 6
- proj_weight: bfloat16 [4096, 128], P('tensor'), may hold values from -0.09375 to 0.09375
- query_reps: bfloat16 [32, 32, 128], P(('groups', 'dp')), parts along dimension 0, may hold values from -6 to 6
- teacher: float32 [32, 256], P(('groups', 'dp')), parts along dimension 0, may hold values from -0.4 to 0.4
- cand_peer: int32 [32, 256, 1], P(('groups', 'dp')), parts along dimension 0, may hold values from 0 to 15; in each aligned block of 256 rows (0 to 255, 256 to 511, ..., all dimensions but the last counted through in order) at most 32 rows name the same one
- cand_doc: int32 [32, 256], P(('groups', 'dp')), parts along dimension 0, may hold values from 0 to 39
- tile_count: int32 [32], P(('groups', 'dp')), parts along dimension 0, may hold values from 1 to 2
- doc_len: int32 [1280], P('groups'), parts along dimension 0, may hold values from 1 to 32
Outputs:
- grad_hidden: bfloat16 [1280, 32, 4096], P(('groups', 'dp'), None, 'tensor'), parts along dimension 0
- grad_weight: float32 [8192, 128], P(('groups', 'tensor')), parts along dimension 0
- grad_query: float32 [32, 32, 128], P(('groups', 'dp')), parts along dimension 0
There are 2 independent parts, one for each index of `groups`. A program takes and returns all parts, laid end to end along the dimension named above; an argument that names none is the same for every part. Nothing has to cross between parts.
Inputs may be any that keep to these rules, and one draw needn't show every extreme that they name: `cand_peer`: in each aligned block of 256 slots (the queries of one dp index) no shard is named more than 32 times; in some block some shard is named exactly 32 times.
All inputs are finite; a program needn't handle non-finite values.
Results may differ from a plain program's by a relative error of at most 0.0077.
Values may be sent and summed in bfloat16 or wider, within the bound.
A program may use at most 128 MiB of HBM per device.

v0:
```python
import math

import jax
import jax.numpy as jnp
from jax import lax
from jax.sharding import PartitionSpec as P

EMB = 128
QT = 32
TILE = 128
SLOTS = 256


token_temp = 0.5
list_temp = 0.2
loss_scale = 4096.0
epsilon = 1e-06


def unit_rows(values):
    factor = lax.rsqrt(jnp.mean(values * values, axis=-1, keepdims=True) + epsilon)
    return (values * factor, factor)


def bucket_positions(peer_rows, shards, capacity):
    onehot = (peer_rows[..., None] == jnp.arange(shards, dtype=jnp.int32)).astype(jnp.int32)
    before = jnp.cumsum(onehot, axis=-2) - onehot
    rank_in = jnp.sum(before * onehot, axis=-1)
    return peer_rows * capacity + rank_in


def smooth_forward(query_rows, doc_rows, token_mask, inv_root):
    similarity = (
        jnp.einsum("bid,bjd->bij", query_rows, doc_rows, preferred_element_type=jnp.float32)
        * inv_root
    )
    weights = jnp.exp(similarity / token_temp) * token_mask[:, None, :]
    return (weights, jnp.sum(weights, axis=-1))


def smooth_backward(weights, totals, score_grad, query_rows, doc_rows, inv_root):
    token_grad = weights / totals[..., None] * (score_grad / QT)[:, None, None]
    token_narrow = token_grad.astype(jnp.bfloat16)
    unit_grad = (
        jnp.einsum("bij,bid->bjd", token_narrow, query_rows, preferred_element_type=jnp.float32)
        * inv_root
    )
    query_part = (
        jnp.einsum("bij,bjd->bid", token_narrow, doc_rows, preferred_element_type=jnp.float32)
        * inv_root
    )
    return (unit_grad, query_part)


def list_gradient(maxsim_slots, teacher, tile_count):
    scores = jnp.mean(maxsim_slots, axis=-1)
    slot_valid = ((jnp.arange(SLOTS) // TILE)[None, :] < tile_count[:, None]).astype(jnp.float32)
    student = jnp.exp(scores / list_temp) * slot_valid
    student = student / jnp.sum(student, axis=-1, keepdims=True)
    target = jnp.exp(teacher) * slot_valid
    target = target / jnp.sum(target, axis=-1, keepdims=True)
    return loss_scale * (student - target) / list_temp


def lengths_mask(lengths, doc_tokens):
    return (jnp.arange(doc_tokens)[None, :] < lengths[:, None]).astype(jnp.float32)


def per_device(
    doc_hidden, proj_weight, query_reps, teacher, cand_peer, cand_doc, tile_count, doc_len
):
    enc_count, doc_tokens, hidden_part = doc_hidden.shape
    shards = lax.axis_size("dp")
    own_queries, slot_count = cand_doc.shape
    capacity = 2 * own_queries * slot_count // shards
    buffer_len = shards * capacity
    inv_root = 1.0 / math.sqrt(EMB)
    flat_hidden = doc_hidden.reshape(enc_count * doc_tokens, hidden_part)
    proj_part = jnp.dot(flat_hidden, proj_weight, preferred_element_type=jnp.float32)
    doc_proj = lax.psum(proj_part, "tensor").reshape(enc_count, doc_tokens, EMB)
    doc_unit, doc_factor = unit_rows(doc_proj)
    doc_narrow = doc_unit.astype(jnp.bfloat16)
    query_unit, query_factor = unit_rows(query_reps.astype(jnp.float32))
    query_narrow = query_unit.astype(jnp.bfloat16)
    own_peers = cand_peer[:, :, 0].reshape(-1)
    own_docs = cand_doc.reshape(-1)
    own_slots = bucket_positions(own_peers[None, :], shards, capacity)[0]
    slot_owner = jnp.arange(own_queries * slot_count, dtype=jnp.int32) // slot_count
    request = jnp.zeros((buffer_len,), jnp.int32).at[own_slots].set(own_docs)
    slot_query = jnp.zeros((buffer_len,), jnp.int32).at[own_slots].set(slot_owner)
    wanted = lax.all_to_all(
        request.reshape(shards, capacity), "dp", split_axis=0, concat_axis=0, tiled=True
    ).reshape(-1)
    served = doc_narrow[wanted].reshape(shards, capacity, doc_tokens, EMB)
    doc_rows = lax.all_to_all(served, "dp", split_axis=0, concat_axis=0, tiled=True).reshape(
        buffer_len, doc_tokens, EMB
    )
    source_shard = jnp.arange(buffer_len, dtype=jnp.int32) // capacity
    token_mask = lengths_mask(doc_len[source_shard * enc_count + request], doc_tokens)
    query_rows = query_narrow[slot_query]
    weights, totals = smooth_forward(query_rows, doc_rows, token_mask, inv_root)
    maxsim = token_temp * jnp.log(totals)
    slot_grads = list_gradient(
        maxsim[own_slots].reshape(own_queries, slot_count, QT), teacher, tile_count
    )
    score_grad = jnp.zeros((buffer_len,), jnp.float32).at[own_slots].set(slot_grads.reshape(-1))
    unit_grad, query_part = smooth_backward(
        weights, totals, score_grad, query_rows, doc_rows, inv_root
    )
    query_pick = (slot_query[:, None] == jnp.arange(own_queries, dtype=jnp.int32)[None, :]).astype(
        jnp.float32
    )
    query_sum = jnp.einsum("bk,bid->kid", query_pick, query_part, precision=lax.Precision.HIGHEST)
    returned = lax.all_to_all(
        unit_grad.reshape(shards, capacity, doc_tokens, EMB),
        "dp",
        split_axis=0,
        concat_axis=0,
        tiled=True,
    ).reshape(buffer_len, doc_tokens, EMB)
    doc_pick = (wanted[:, None] == jnp.arange(enc_count, dtype=jnp.int32)[None, :]).astype(
        jnp.float32
    )
    doc_grad = jnp.einsum("bn,bjd->njd", doc_pick, returned, precision=lax.Precision.HIGHEST)
    proj_grad = doc_factor * (
        doc_grad - doc_unit * jnp.mean(doc_unit * doc_grad, axis=-1, keepdims=True)
    )
    proj_narrow = proj_grad.astype(jnp.bfloat16).reshape(enc_count * doc_tokens, EMB)
    grad_hidden = lax.dot_general(
        proj_narrow, proj_weight, (((1,), (1,)), ((), ())), preferred_element_type=jnp.float32
    ).astype(jnp.bfloat16)
    grad_hidden = grad_hidden.reshape(enc_count, doc_tokens, hidden_part)
    weight_part = lax.dot_general(
        flat_hidden, proj_narrow, (((0,), (0,)), ((), ())), preferred_element_type=jnp.float32
    )
    grad_weight = lax.psum(weight_part, "dp") / (enc_count * shards)
    grad_query = query_factor * (
        query_sum - query_unit * jnp.mean(query_unit * query_sum, axis=-1, keepdims=True)
    )
    return (grad_hidden, grad_weight, grad_query)


def solution(mesh):
    placed = (
        P(("groups", "dp"), None, "tensor"),
        P("tensor", None),
        P(("groups", "dp"), None, None),
        P(("groups", "dp"), None),
        P(("groups", "dp"), None, None),
        P(("groups", "dp"), None),
        P(("groups", "dp")),
        P("groups"),
    )
    return jax.shard_map(
        per_device,
        mesh=mesh,
        in_specs=placed,
        out_specs=(
            P(("groups", "dp"), None, "tensor"),
            P(("groups", "tensor"), None),
            P(("groups", "dp"), None, None),
        ),
        check_vma=False,
    )
```

profile of v0, /device:TPU:1, one launch (start us, length us, event | category | flops | bytes accessed | tf_op | source)
XLA Modules:
  0.0 458.6 jit_solution(18067374805940954504)
XLA Ops:
  7.2 0.8 compare_convert_fusion
  9.0 0.7 fusion.20
  9.7 0.7 compare_select_fusion.2
  10.4 1.6 scatter_custom_fusion
  12.0 0.7 all_to_all.12
  12.6 7.3 %all-to-all-start = ((s32[16,1,32]{2,1,0:T(1,128)}), s32[16,1,32]{2,1,0:T(1,128)S(1)}, u32[]{:S(2)}, u32[]{:S(2)}) async-start(s32[16,1,32]{2,1,0:T(1,128)} %all_to_all.12), calls=%async_computation | async-start | bytes 16384 | tf_op jit(solution)/shard_map/all_to_all | solution.py:91
  20.0 5.7 %multiply_reduce_fusion.1 = (f32[40,32]{1,0:T(8,128)S(1)}, f32[40,32,128]{2,1,0:T(8,128)S(1)}) fusion(bf16[40,32,4096]{2,1,0:T(8,128)(2,1)} %param.8, bf16[4096,128]{1,0:T(8,128)(2,1)S(1)} %copy-done), kind=kOutput, calls=%fused_computation.23 | convolution fusion | flops 1342503680 | bytes 12194816 | tf_op jit(solution)/shard_map/dot_general | solution.py:79
  26.1 3.5 gather_fusion
  29.6 6.0 %all-to-all-start.1 = ((bf16[16,32,32,128]{3,2,1,0:T(8,128)(2,1)}), bf16[16,32,32,128]{3,2,1,0:T(8,128)(2,1)}, u32[]{:S(2)}, u32[]{:S(2)}) async-start(bf16[16,32,32,128]{3,2,1,0:T(8,128)(2,1)} %bitcast.69), calls=%async_computation.1 | async-start | bytes 8388608 | tf_op jit(solution)/shard_map/all_to_all | solution.py:95
  36.3 2.3 gather_fusion.1
  38.8 0.7 fusion.36
  39.7 74.0 %all-to-all-done.1 = bf16[16,32,32,128]{3,2,1,0:T(8,128)(2,1)} async-done(((bf16[16,32,32,128]{3,2,1,0:T(8,128)(2,1)}), bf16[16,32,32,128]{3,2,1,0:T(8,128)(2,1)}, u32[]{:S(2)}, u32[]{:S(2)}) %all-to-all-start.1) | async-done | bytes 4194336 | tf_op jit(solution)/shard_map/all_to_all | solution.py:95
  113.7 7.4 %fusion.2 = (f32[512,32]{1,0:T(8,128)S(1)}, f32[512,32,32]{1,2,0:T(8,128)}) fusion(f32[512,32]{1,0:T(8,128)S(1)} %fusion.8, bf16[512,32,128]{2,1,0:T(8,128)(2,1)} %bitcast.16, bf16[32,128]{1,0:T(8,128)(2,1)S(1)} %fusion.21), kind=kOutput, calls=%fused_computation.11 | convolution fusion | flops 135774208 | bytes 6430720 | tf_op jit(solution)/shard_map/bid,bjd->bij/dot_general | solution.py:34
  121.2 0.7 gather_fusion.2
  122.0 0.6 fusion.34
  122.6 1.3 fusion.35
  124.0 1.4 scatter_custom_fusion.2
  125.4 8.7 %broadcast_multiply_fusion.1 = f32[512,32,128]{2,1,0:T(8,128)} fusion(bf16[32,128]{1,0:T(8,128)(2,1)S(1)} %fusion.21, f32[512,32,32]{1,2,0:T(8,128)} %get-tuple-element.14, f32[512]{0:T(512)S(1)} %broadcast_multiply_fusion.4, f32[512,32]{1,0:T(8,128)S(1)} %get-tuple-element.13, f32[512,32]{1,0:T(8,128)S(1)} %fusion.8), kind=kOutput, calls=%fused_computation.14 | convolution fusion | flops 138936320 | bytes 10627072 | tf_op jit(solution)/shard_map/bij,bid->bjd/dot_general | solution.py:45
  134.1 19.3 %all-to-all-start.2 = ((f32[16,32,32,128]{3,2,1,0:T(8,128)}), f32[16,32,32,128]{3,2,1,0:T(8,128)}, u32[]{:S(2)}, u32[]{:S(2)}) async-start(f32[16,32,32,128]{3,2,1,0:T(8,128)} %bitcast.70), calls=%async_computation.2 | async-start | bytes 16777216 | tf_op jit(solution)/shard_map/all_to_all | solution.py:114
  153.5 1.4 scatter_custom_fusion.1
  155.4 0.7 reduce.15
  156.2 8.4 %broadcast_multiply_fusion = f32[512,32,128]{2,1,0:T(8,128)S(1)} fusion(bf16[512,32,128]{2,1,0:T(8,128)(2,1)} %bitcast.16, f32[512,32,32]{1,2,0:T(8,128)} %get-tuple-element.14, f32[512]{0:T(512)S(1)} %broadcast_multiply_fusion.4, f32[512,32]{1,0:T(8,128)S(1)} %get-tuple-element.13, f32[512,32]{1,0:T(8,128)S(1)} %fusion.8), kind=kOutput, calls=%fused_computation.13 | convolution fusion | flops 138936320 | bytes 14813184 | tf_op jit(solution)/shard_map/bij,bjd->bid/dot_general | solution.py:49
  164.5 7.5 %fusion = f32[1,32,128]{2,0,1:T(1,128)S(1)} fusion(pred[512,1,1]{0,1,2:T(4,128)(4,1)S(1)} %reshape.431, f32[512,32,128]{2,1,0:T(8,128)S(1)} %broadcast_multiply_fusion), kind=kOutput, calls=%fused_computation.7 | convolution fusion | flops 25165824 | bytes 8405504 | tf_op jit(solution)/shard_map/bk,bid->kid/dot_general | solution.py:113
  172.0 132.5 %all-to-all-done.2 = f32[16,32,32,128]{3,2,1,0:T(8,128)} async-done(((f32[16,32,32,128]{3,2,1,0:T(8,128)}), f32[16,32,32,128]{3,2,1,0:T(8,128)}, u32[]{:S(2)}, u32[]{:S(2)}) %all-to-all-start.2) | async-done | bytes 8388640 | tf_op jit(solution)/shard_map/all_to_all | solution.py:114
  304.5 8.6 %copy.20 = f32[16,32,32,128]{3,1,0,2:T(8,128)S(1)} copy(f32[16,32,32,128]{3,2,1,0:T(8,128)} %all-to-all-done.2) | data formatting | bytes 16777216 | tf_op jit(solution)/shard_map/all_to_all | solution.py:114
  313.2 3.2 fusion.10
  317.3 2.9 convolution_bitcast_fusion
  320.4 0.7 fusion.18
  321.1 5.6 %convolution_convert_fusion = bf16[1280,4096]{1,0:T(8,128)(2,1)} fusion(bf16[1280,128]{1,0:T(8,128)(2,1)S(1)} %bitcast.71, bf16[4096,128]{1,0:T(8,128)(2,1)S(1)} %copy-done), kind=kOutput, calls=%fused_computation.6 | convolution fusion | flops 1347420160 | bytes 11862016 | tf_op jit(solution)/shard_map/dot_general | solution.py:129
  326.7 121.4 %all-reduce.2.cloned.1.call-done = f32[4096,128]{0,1:T(8,128)} async-done(((f32[4096,128]{0,1:T(8,128)}), f32[4096,128]{0,1:T(8,128)}) %all-reduce.2.cloned.1.call-update) | async-done | bytes 2097168 | tf_op jit(solution)/shard_map/psum | solution.py:136
  448.2 1.8 broadcast_multiply_fusion.2
  449.9 1.8 copy.25
  (51 shorter events, 3.6 us)
Async XLA Ops:
  7.2 12.8 %copy-start = (bf16[4096,128]{1,0:T(8,128)(2,1)S(1)}, bf16[4096,128]{1,0:T(8,128)(2,1)}, u32[]{:S(2)}) copy-start(bf16[4096,128]{1,0:T(8,128)(2,1)} %param.9) | copy-start | bytes 3145732
  12.6 13.3 %all-to-all-start = ((s32[16,1,32]{2,1,0:T(1,128)}), s32[16,1,32]{2,1,0:T(1,128)S(1)}, u32[]{:S(2)}, u32[]{:S(2)}) async-start(s32[16,1,32]{2,1,0:T(1,128)} %all_to_all.12), calls=%async_computation | async-start | bytes 16384 | tf_op jit(solution)/shard_map/all_to_all | solution.py:91
  26.1 10.2 %copy-start.1 = (s32[640]{0:T(1024)S(1)}, s32[640]{0:T(1024)}, u32[]{:S(2)}) copy-start(s32[640]{0:T(1024)} %param.15) | copy-start | bytes 7684
  26.1 12.6 %copy-start.2 = (bf16[1,32,128]{2,1,0:T(8,128)(2,1)S(1)}, bf16[1,32,128]{2,1,0:T(8,128)(2,1)}, u32[]{:S(2)}) copy-start(bf16[1,32,128]{2,1,0:T(8,128)(2,1)} %param.10) | copy-start | bytes 24580
  26.1 12.7 %copy-start.3 = (f32[1,256]{1,0:T(1,128)S(1)}, f32[1,256]{1,0:T(1,128)}, u32[]{:S(2)}) copy-start(f32[1,256]{1,0:T(1,128)} %param.11) | copy-start | bytes 3076
  29.6 84.1 %all-to-all-start.1 = ((bf16[16,32,32,128]{3,2,1,0:T(8,128)(2,1)}), bf16[16,32,32,128]{3,2,1,0:T(8,128)(2,1)}, u32[]{:S(2)}, u32[]{:S(2)}) async-start(bf16[16,32,32,128]{3,2,1,0:T(8,128)(2,1)} %bitcast.69), calls=%async_computation.1 | async-start | bytes 8388608 | tf_op jit(solution)/shard_map/all_to_all | solution.py:95
  134.1 170.4 %all-to-all-start.2 = ((f32[16,32,32,128]{3,2,1,0:T(8,128)}), f32[16,32,32,128]{3,2,1,0:T(8,128)}, u32[]{:S(2)}, u32[]{:S(2)}) async-start(f32[16,32,32,128]{3,2,1,0:T(8,128)} %bitcast.70), calls=%async_computation.2 | async-start | bytes 16777216 | tf_op jit(solution)/shard_map/all_to_all | solution.py:114
  153.4 294.7 %all-reduce.2.cloned.1.call-start = ((), (), s32[]{:S(2)}) async-start(), calls=%async_computation.3 | async-start | bytes 4194304 | tf_op jit(solution)/shard_map/psum | solution.py:136
  304.5 12.7 %slice-start = ((s8[10485760]{0:T(1024)(128)(4,1)}), s8[4194304]{0:T(1024)(128)(4,1)S(1)}, s32[]{:S(2)}) async-start(s8[10485760]{0:T(1024)(128)(4,1)} %bitcast.67), calls=%async_computation.4 | async-start | bytes 8388608
  304.5 12.8 %slice-start.1 = ((s8[10485760]{0:T(1024)(128)(4,1)}), s8[4194304]{0:T(1024)(128)(4,1)S(1)}, s32[]{:S(2)}) async-start(s8[10485760]{0:T(1024)(128)(4,1)} %bitcast.67), calls=%async_computation.5 | async-start | bytes 8388608
  313.1 4.2 slice-start.2
Sparse Core Ops, SparseCore 0:
  320.3 127.7 all-reduce.1
where the time goes:
time: 461 us; the launch traced here: 459 us
  waiting for transfers between devices  328 us (71%)
  matrix products  49.4 us (11%)
  starting transfers between devices  32.7 us (7%)
  local copies, waits for them, and re-layouts  23.1 us (5%)
  between operations  15 us (3%)
  other arithmetic  10.4 us (2%)
    all_to_all x1, waiting for transfers between devices, per_device(): lax.all_to_all(unit_grad.reshape(shards, capacity, doc_tokens, EMB), 'dp'...  133 us
    psum x1, waiting for transfers between devices, per_device(): grad_weight = lax.psum(weight_part, 'dp') / (enc_count * shards)  121 us
    all_to_all x1, waiting for transfers between devices, per_device(): lax.all_to_all(served, 'dp', split_axis=0, concat_axis=0, tiled=True)  74 us
    all_to_all x1, starting transfers between devices, per_device(): lax.all_to_all(unit_grad.reshape(shards, capacity, doc_tokens, EMB), 'dp'...  19.3 us
  transfers between devices with their start and end apart: 4, of which 3 were waited for; matrix products, arithmetic and copies ran while one was open for 7% of the time, Pallas kernels for 0%

commit v1 on v0

v1 whole, which is shorter than its diff:
```python
import math

import jax
import jax.numpy as jnp
from jax import lax
from jax.sharding import PartitionSpec as P

EMB = 128
QT = 32
TILE = 128

token_temp = 0.5
list_temp = 0.2
loss_scale = 4096.0
epsilon = 1e-06


def unit_rows(values):
    factor = lax.rsqrt(jnp.mean(values * values, axis=-1, keepdims=True) + epsilon)
    return (values * factor, factor)


def list_tables(teacher, cand_peer, cand_doc, tile_count, shards, enc_count):
    slot_count = cand_doc.shape[1]
    valid = (jnp.arange(slot_count)[None, :] // TILE < tile_count[:, None]).astype(jnp.float32)
    target = jnp.exp(teacher) * valid
    target = target / jnp.sum(target, axis=-1, keepdims=True)
    ident = cand_peer[:, :, 0] * enc_count + cand_doc
    named = ident[:, :, None] == jnp.arange(shards * enc_count, dtype=jnp.int32)[None, None, :]
    count = jnp.sum(jnp.where(named, valid[:, :, None], 0.0), axis=1)
    wanted = jnp.sum(jnp.where(named, target[:, :, None], 0.0), axis=1)
    return count, wanted


def with_collectives(
    doc_hidden, proj_weight, query_reps, teacher, cand_peer, cand_doc, tile_count, doc_len
):
    enc_count, doc_tokens, hidden_part = doc_hidden.shape
    shards = lax.axis_size("dp")
    me = lax.axis_index("dp")
    inv_root = 1.0 / math.sqrt(EMB)
    query_unit, query_factor = unit_rows(query_reps.astype(jnp.float32))
    query_narrow = query_unit.astype(jnp.bfloat16)
    count, wanted = list_tables(teacher, cand_peer, cand_doc, tile_count, shards, enc_count)
    every_query = lax.all_gather(query_narrow, "dp", axis=0, tiled=True)
    tables = lax.all_gather(jnp.stack([count, wanted], axis=1), "dp", axis=0, tiled=True)
    tables = lax.dynamic_slice_in_dim(tables, me * enc_count, enc_count, axis=2)
    count, wanted = tables[:, 0], tables[:, 1]
    flat_hidden = doc_hidden.reshape(enc_count * doc_tokens, hidden_part)
    proj_part = jnp.dot(flat_hidden, proj_weight, preferred_element_type=jnp.float32)
    doc_proj = lax.psum(proj_part, "tensor").reshape(enc_count, doc_tokens, EMB)
    doc_unit, doc_factor = unit_rows(doc_proj)
    doc_narrow = doc_unit.astype(jnp.bfloat16)
    own_len = lax.dynamic_slice_in_dim(doc_len, me * enc_count, enc_count)
    token_mask = (jnp.arange(doc_tokens)[None, :] < own_len[:, None]).astype(jnp.float32)
    similarity = (
        jnp.einsum("qid,ejd->qiej", every_query, doc_narrow, preferred_element_type=jnp.float32)
        * inv_root
    )
    weights = jnp.exp(similarity / token_temp) * token_mask
    totals = jnp.sum(weights, axis=-1)
    scores = jnp.mean(token_temp * jnp.log(totals), axis=1)
    raised = jnp.exp(scores / list_temp) * count
    norm = lax.psum(jnp.sum(raised, axis=-1), "dp")
    score_grad = loss_scale * (raised / norm[:, None] - wanted) / list_temp
    token_grad = weights / totals[..., None] * (score_grad / QT)[:, None, :, None]
    token_narrow = token_grad.astype(jnp.bfloat16)
    doc_grad = (
        jnp.einsum("qiej,qid->ejd", token_narrow, every_query, preferred_element_type=jnp.float32)
        * inv_root
    )
    query_part = (
        jnp.einsum("qiej,ejd->qid", token_narrow, doc_narrow, preferred_element_type=jnp.float32)
        * inv_root
    )
    query_sum = lax.psum_scatter(query_part, "dp", scatter_dimension=0, tiled=True)
    proj_grad = doc_factor * (
        doc_grad - doc_unit * jnp.mean(doc_unit * doc_grad, axis=-1, keepdims=True)
    )
    proj_narrow = proj_grad.astype(jnp.bfloat16).reshape(enc_count * doc_tokens, EMB)
    grad_hidden = lax.dot_general(
        proj_narrow, proj_weight, (((1,), (1,)), ((), ())), preferred_element_type=jnp.float32
    ).astype(jnp.bfloat16)
    grad_hidden = grad_hidden.reshape(enc_count, doc_tokens, hidden_part)
    weight_part = lax.dot_general(
        flat_hidden, proj_narrow, (((0,), (0,)), ((), ())), preferred_element_type=jnp.float32
    )
    grad_weight = lax.psum(weight_part, "dp") / (enc_count * shards)
    grad_query = query_factor * (
        query_sum - query_unit * jnp.mean(query_unit * query_sum, axis=-1, keepdims=True)
    )
    return (grad_hidden, grad_weight, grad_query)


def solution(mesh):
    placed = (
        P(("groups", "dp"), None, "tensor"),
        P("tensor", None),
        P(("groups", "dp"), None, None),
        P(("groups", "dp"), None),
        P(("groups", "dp"), None, None),
        P(("groups", "dp"), None),
        P(("groups", "dp")),
        P("groups"),
    )
    return jax.shard_map(
        with_collectives,
        mesh=mesh,
        in_specs=placed,
        out_specs=(
            P(("groups", "dp"), None, "tensor"),
            P(("groups", "tensor"), None),
            P(("groups", "dp"), None, None),
        ),
        check_vma=False,
    )
```

time: 461 us -> 270 us (0.59)
  waiting for transfers between devices: 328 us -> 135 us
  blocking collectives: 0 us -> 70 us
  starting transfers between devices: 32.7 us -> 0.26 us
  matrix products: 49.4 us -> 28.9 us
  local copies, waits for them, and re-layouts: 23.1 us -> 4.7 us
    all_to_all x3 -> x0, waiting for transfers between devices: 207 us -> none  [the longest x1 133 us: per_device(): lax.all_to_all(unit_grad.reshape(shards, capacity, doc_tokens, EMB), 'dp'...]
    all_gather x0 -> x2, blocking collectives: none -> 41 us  [the longest x1 23.2 us: with_collectives(): lax.all_gather(jnp.stack([count, wanted], axis=1), 'dp', axis=0, tiled=True)]
    reduce_scatter x0 -> x1, waiting for transfers between devices: none -> 35.2 us  [with_collectives(): lax.psum_scatter(query_part, 'dp', scatter_dimension=0, tiled=True)]
    all_to_all x3 -> x0, starting transfers between devices: 32.7 us -> none  [the longest x1 19.3 us: per_device(): lax.all_to_all(unit_grad.reshape(shards, capacity, doc_tokens, EMB), 'dp'...]
    psum x0 -> x1, blocking collectives: none -> 29 us  [with_collectives(): norm = lax.psum(jnp.sum(raised, axis=-1), 'dp')]
    psum x1, waiting for transfers between devices: 121 us -> 99.8 us  [with_collectives(): grad_weight = lax.psum(weight_part, 'dp') / (enc_count * shards)]
    dot_general x8 -> x6, matrix products: 49.4 us -> 28.9 us  [the longest x1 6.93 us: with_collectives(): lax.dot_general(flat_hidden, proj_narrow, (((0,), (0,)), ((), ())), prefe...]
    all_to_all x3 -> x0, local copies, waits for them, and re-layouts: 9.8 us -> none  [the longest x1 8.6 us: per_device(): lax.all_to_all(unit_grad.reshape(shards, capacity, doc_tokens, EMB), 'dp'...]
  transfers between devices with their start and end apart: 4 -> 2, of which waited for: 3 -> 2; matrix products, arithmetic and copies ran while one was open for 7% -> 7% of each run, Pallas kernels for 0% -> 0%
where the time goes in v1:
time: 270 us; the launch traced here: 268 us
  waiting for transfers between devices  135 us (50%)
  blocking collectives  70 us (26%)
  matrix products  28.9 us (11%)
  between operations  14.9 us (6%)
  other arithmetic  14.4 us (5%)
  local copies, waits for them, and re-layouts  4.7 us (2%)
    psum x1, waiting for transfers between devices, with_collectives(): grad_weight = lax.psum(weight_part, 'dp') / (enc_count * shards)  99.8 us
    reduce_scatter x1, waiting for transfers between devices, with_collectives(): lax.psum_scatter(query_part, 'dp', scatter_dimension=0, tiled=True)  35.2 us
    psum x1, blocking collectives, with_collectives(): norm = lax.psum(jnp.sum(raised, axis=-1), 'dp')  29 us
    all_gather x1, blocking collectives, with_collectives(): lax.all_gather(jnp.stack([count, wanted], axis=1), 'dp', axis=0, tiled=True)  23.2 us
    all_gather x1, blocking collectives, with_collectives(): every_query = lax.all_gather(query_narrow, 'dp', axis=0, tiled=True)  17.8 us
    dot_general x1, matrix products, with_collectives(): lax.dot_general(flat_hidden, proj_narrow, (((0,), (0,)), ((), ())), prefe...  6.93 us
    dot_general x1, matrix products, with_collectives(): jnp.dot(flat_hidden, proj_weight, preferred_element_type=jnp.float32)  5.68 us
    dot_general x1, matrix products, with_collectives(): lax.dot_general(proj_narrow, proj_weight, (((1,), (1,)), ((), ())), prefe...  5.64 us
  transfers between devices with their start and end apart: 2, of which 2 were waited for; matrix products, arithmetic and copies ran while one was open for 7% of the time, Pallas kernels for 0%

profile of v1, /device:TPU:1, one launch (start us, length us, event | category | flops | bytes accessed | tf_op | source)
XLA Modules:
  0.0 268.2 jit_solution(15549315430778403779)
XLA Ops:
  8.0 0.8 fusion.17
  8.8 0.7 bitcast_add_fusion
  9.5 1.3 fusion.20
  10.8 0.6 broadcast_divide_fusion
  11.4 0.2 select_reduce_fusion.1
  11.7 0.8 fusion.13
  12.4 0.8 dynamic_slice.6
  13.2 23.2 %all_gather.7 = f32[16,2,640]{2,1,0:T(2,128)S(1)} all-gather(f32[1,2,640]{2,1,0:T(2,128)S(1)} %pad_maximum_fusion), channel_id=1, replica_groups=mesh['groups'=2,'dp'=16,'tensor'=1] {'dp'}, dimensions={0}, use_global_device_ids=true | all-gather | bytes 87040 | tf_op jit(solution)/shard_map/all_gather | solution.py:46
  36.4 17.8 %all_gather.6 = bf16[16,32,128]{2,1,0:T(8,128)(2,1)S(1)} all-gather(bf16[1,32,128]{2,1,0:T(8,128)(2,1)S(1)} %fusion.13), channel_id=1, replica_groups=mesh['groups'=2,'dp'=16,'tensor'=1] {'dp'}, dimensions={0}, use_global_device_ids=true | all-gather | bytes 139264 | tf_op jit(solution)/shard_map/all_gather | solution.py:45
  54.2 5.7 %multiply_reduce_fusion.1 = (f32[40,32]{1,0:T(8,128)S(1)}, f32[40,32,128]{2,1,0:T(8,128)S(1)}) fusion(bf16[40,32,4096]{2,1,0:T(8,128)(2,1)} %param.8, bf16[4096,128]{1,0:T(8,128)(2,1)S(1)} %copy-done), kind=kOutput, calls=%fused_computation.17 | convolution fusion | flops 1342503680 | bytes 12194816 | tf_op jit(solution)/shard_map/dot_general | solution.py:50
  59.9 0.2 multiply_convert_fusion.2
  60.1 5.5 %fusion = (f32[16,32,40]{2,1,0:T(8,128)S(1)}, f32[16,32,40,32]{2,1,3,0:T(8,128)}) fusion(f32[40,32]{0,1:T(8,128)S(1)} %fusion.18, bf16[40,32,128]{2,1,0:T(8,128)(2,1)S(1)} %multiply_convert_fusion.2, bf16[16,32,128]{2,1,0:T(8,128)(2,1)S(1)} %all_gather.6), kind=kOutput, calls=%fused_computation.3 | convolution fusion | flops 169717760 | bytes 3167232 | tf_op jit(solution)/shard_map/qid,ejd->qiej/dot_general | solution.py:57
  65.6 0.1 multiply_reduce_fusion.2
  65.7 0.1 constant_dynamic-slice_fusion
  65.8 0.1 fusion.19
  65.9 29.0 %psum.14 = f32[16]{0:T(128)S(1)} all-reduce(f32[16]{0:T(128)S(1)} %fusion.19), channel_id=1, replica_groups=mesh['groups'=2,'dp'=16,'tensor'=1] {'dp'}, use_global_device_ids=true, to_apply=%region_8.9 | all-reduce | flops 16 | bytes 128 | tf_op jit(solution)/shard_map/psum | solution.py:64
  94.9 0.1 subtract_multiply_fusion
  95.0 4.6 %multiply_convert_fusion = bf16[16,32,40,32]{2,1,3,0:T(8,128)(2,1)S(1)} fusion(f32[16,32,40,32]{2,1,3,0:T(8,128)} %get-tuple-element.21, f32[16,40]{1,0:T(8,128)S(1)} %subtract_multiply_fusion, f32[16,32,40]{2,1,0:T(8,128)S(1)} %get-tuple-element.20, f32[40,32]{0,1:T(8,128)S(1)} %fusion.18), kind=kLoop, calls=%fused_computation.1 | loop fusion | flops 3276800 | bytes 4021760 | tf_op jit(solution)/shard_map/convert_element_type | solution.py:67
  99.6 2.0 copy-done.1
  101.6 1.7 fusion.1
  103.3 0.2 all-reduce.2.cloned.1.call-start
  103.6 3.4 %convolution_bitcast_fusion.1 = f32[40,32,128]{2,0,1:T(8,128)S(1)} fusion(bf16[16,32,40,32]{2,1,3,0:T(8,128)(2,1)} %copy-done.1, bf16[16,32,128]{2,1,0:T(8,128)(2,1)S(1)} %all_gather.6), kind=kOutput, calls=%fused_computation.5 | convolution fusion | flops 167772160 | bytes 2097152 | tf_op jit(solution)/shard_map/qiej,qid->ejd/dot_general | solution.py:69
  107.0 0.5 multiply_reduce_fusion
  107.5 0.4 multiply_convert_fusion.1
  107.9 6.9 %convolution_bitcast_fusion = f32[4096,128]{0,1:T(8,128)} fusion(bf16[40,32,128]{2,1,0:T(8,128)(2,1)S(1)} %multiply_convert_fusion.1, bf16[40,32,4096]{2,1,0:T(8,128)(2,1)} %param.8), kind=kOutput, calls=%fused_computation.4 | convolution fusion | flops 1342177280 | bytes 12910592 | tf_op jit(solution)/shard_map/dot_general | solution.py:85
  114.9 5.6 %convolution_convert_fusion = bf16[1280,4096]{1,0:T(8,128)(2,1)} fusion(bf16[1280,128]{1,0:T(8,128)(2,1)S(1)} %bitcast.54, bf16[4096,128]{1,0:T(8,128)(2,1)S(1)} %copy-done), kind=kOutput, calls=%fused_computation | convolution fusion | flops 1347420160 | bytes 11862016 | tf_op jit(solution)/shard_map/dot_general | solution.py:81
  120.5 35.2 %reduce-scatter.2.cloned.1.call-done = f32[1,32,128]{2,1,0:T(8,128)} async-done(((f32[16,32,128]{2,1,0:T(8,128)}), f32[1,32,128]{2,1,0:T(8,128)}) %reduce-scatter.2.cloned.1.call-update) | async-done | bytes 16400 | tf_op jit(solution)/shard_map/reduce_scatter | solution.py:76
  155.7 0.9 fusion.14
  156.6 1.4 fusion.16
  158.0 99.8 %all-reduce.2.cloned.1.call-done = f32[4096,128]{0,1:T(8,128)} async-done(((f32[4096,128]{0,1:T(8,128)}), f32[4096,128]{0,1:T(8,128)}) %all-reduce.2.cloned.1.call-update) | async-done | bytes 2097168 | tf_op jit(solution)/shard_map/psum | solution.py:88
  257.8 1.8 broadcast_multiply_fusion
  259.6 1.8 copy.28
  (17 shorter events, 0.2 us)
Async XLA Ops:
  7.2 47.0 %copy-start = (bf16[4096,128]{1,0:T(8,128)(2,1)S(1)}, bf16[4096,128]{1,0:T(8,128)(2,1)}, u32[]{:S(2)}) copy-start(bf16[4096,128]{1,0:T(8,128)(2,1)} %param.9) | copy-start | bytes 3145732
  7.2 148.5 %reduce-scatter.2.cloned.1.call-start = ((), (), s32[]{:S(2)}) async-start(), calls=%async_computation.2 | async-start | bytes 278528 | tf_op jit(solution)/shard_map/reduce_scatter | solution.py:76
  99.6 2.0 copy-start.1
  103.3 154.4 %all-reduce.2.cloned.1.call-start = ((), (), s32[]{:S(2)}) async-start(), calls=%async_computation.1 | async-start | bytes 4194304 | tf_op jit(solution)/shard_map/psum | solution.py:88
  114.9 40.8 %copy-start.2 = (bf16[1,32,128]{2,1,0:T(8,128)(2,1)S(1)}, bf16[1,32,128]{2,1,0:T(8,128)(2,1)}, u32[]{:S(2)}) copy-start(bf16[1,32,128]{2,1,0:T(8,128)(2,1)} %param.10) | copy-start | bytes 24580
Sparse Core Ops, SparseCore 0:
  103.5 52.1 reduce-scatter.1
  159.8 97.9 all-reduce.1

commit v2 on v1

--- a/solution.py
+++ b/solution.py
@@ -1,8 +1,11 @@
+import functools
 import math
 
 import jax
 import jax.numpy as jnp
 from jax import lax
+from jax.experimental import pallas as pl
+from jax.experimental.pallas import tpu as pltpu
 from jax.sharding import PartitionSpec as P
 
 EMB = 128
@@ -92,7 +95,473 @@
     return (grad_hidden, grad_weight, grad_query)
 
 
+HIGH = lax.Precision.HIGHEST
+MESH = pl.DeviceIdType.MESH
+
+
+def grid_of(shape, dim):
+    return lax.broadcasted_iota(jnp.int32, shape, dim)
+
+
+def exchange_kernel(
+    shards,
+    enc_count,
+    doc_tokens,
+    hidden_hbm,
+    weight_hbm,
+    query_ref,
+    list_ref,
+    length_ref,
+    narrow_ref,
+    gathered_ref,
+    query_grad_ref,
+    hidden,
+    weight,
+    unit,
+    factor,
+    doc_narrow,
+    weights,
+    totals,
+    token_narrow,
+    narrow_t,
+    queries,
+    table_out,
+    table_in,
+    norms,
+    part_out,
+    part_in,
+    pair_out,
+    pair_in,
+    chip_out,
+    chip_in,
+    own_sum,
+    load_sem,
+    query_send,
+    query_recv,
+    table_send,
+    table_recv,
+    norm_send,
+    norm_recv,
+    part_send,
+    part_recv,
+    pair_send,
+    pair_recv,
+    chip_send,
+    chip_recv,
+    ring_send,
+    ring_recv,
+    mate_send,
+    mate_recv,
+):
+    f32, bf16 = jnp.float32, jnp.bfloat16
+    me = lax.axis_index("dp")
+    core = lax.rem(me, 2)
+    chip = lax.div(me, 2)
+    chips = shards // 2
+    mate = chip * 2 + (1 - core)
+    inv_root = 1.0 / math.sqrt(EMB)
+    tokens, hid = hidden.shape
+    lanes = shards * QT
+    docs = 8
+    block = docs * doc_tokens
+    blocks = tokens // block
+    chunk = hid // shards
+
+    weight_copy = pltpu.make_async_copy(weight_hbm, weight, load_sem.at[blocks])
+    weight_copy.start()
+
+    def hidden_copy(b):
+        rows = pl.ds(pl.multiple_of(b * block, block), block)
+        return pltpu.make_async_copy(hidden_hbm.at[rows], hidden.at[rows], load_sem.at[b])
+
+    for b in range(blocks):
+        hidden_copy(b).start()
+
+    barrier = pltpu.get_barrier_semaphore()
+    for t in range(1, shards):
+        pl.semaphore_signal(
+            barrier, inc=1, device_id={"dp": lax.rem(me + t, shards)}, device_id_type=MESH
+        )
+
+    def remote(src, dst, send, recv, peer):
+        return pltpu.make_async_remote_copy(
+            src_ref=src,
+            dst_ref=dst,
+            send_sem=send,
+            recv_sem=recv,
+            device_id={"dp": peer},
+            device_id_type=MESH,
+        )
+
+    query = query_ref[...].astype(f32)
+    query_factor = lax.rsqrt(jnp.mean(query * query, axis=-1, keepdims=True) + epsilon)
+    query_unit = query * query_factor
+    queries[me] = query_unit.astype(bf16)
+    slots = list_ref.shape[1]
+    valid = list_ref[1:2, :]
+    target = jnp.exp(list_ref[0:1, :]) * valid
+    target = target / jnp.sum(target, axis=-1, keepdims=True)
+    ident = list_ref[2:3, :]
+    row = grid_of((8, slots), 0)
+    terms = jnp.where(row == 0, valid, jnp.where(row == 1, target, 0.0))
+    for p in range(shards):
+        named = (grid_of((EMB, slots), 0) + p * EMB).astype(f32) == ident
+        table_out[p] = lax.dot_general(
+            terms,
+            jnp.where(named, 1.0, 0.0),
+            (((1,), (1,)), ((), ())),
+            precision=HIGH,
+            preferred_element_type=f32,
+        )
+    table_in[me] = table_out[me]
+
+    pl.semaphore_wait(barrier, shards - 1)
+    first = []
+    for t in range(1, shards):
+        peer = lax.rem(me + t, shards)
+        first.append(
+            remote(queries.at[me], queries.at[me], query_send.at[t], query_recv.at[t], peer)
+        )
+        first.append(
+            remote(table_out.at[peer], table_in.at[me], table_send.at[t], table_recv.at[t], peer)
+        )
+    for copy in first:
+        copy.start()
+
+    weight_copy.wait()
+
+    def project(b, carry):
+        hidden_copy(b).wait()
+        rows = pl.ds(pl.multiple_of(b * block, block), block)
+        proj = jnp.dot(hidden[rows], weight[...], preferred_element_type=f32)
+        scale = lax.rsqrt(jnp.mean(proj * proj, axis=-1, keepdims=True) + epsilon)
+        values = proj * scale
+        unit[rows] = values
+        factor[rows] = jnp.broadcast_to(scale, values.shape)
+        doc_narrow[rows] = values.astype(bf16)
+        return carry
+
+    lax.fori_loop(0, blocks, project, 0)
+
+    for copy in first:
+        copy.wait_recv()
+    every = queries[...].reshape(lanes, EMB)
+
+    def score(b, carry):
+        rows = pl.ds(pl.multiple_of(b * block, block), block)
+        some = pl.ds(pl.multiple_of(b * docs, docs), docs)
+        product = lax.dot_general(
+            doc_narrow[rows], every, (((1,), (1,)), ((), ())), preferred_element_type=f32
+        )
+        grown = jnp.exp(product * (inv_root / token_temp)).reshape(docs, doc_tokens, lanes)
+        inside = grid_of((docs, doc_tokens, lanes), 1).astype(f32) < length_ref[some][:, None, :]
+        grown = jnp.where(inside, grown, 0.0)
+        weights[rows] = grown.reshape(block, lanes)
+        totals[some] = jnp.sum(grown, axis=1)
+        return carry
+
+    lax.fori_loop(0, blocks, score, 0)
+
+    table = table_in[...].reshape(shards * 8, EMB)
+    place = grid_of((shards * 8, lanes), 0)
+    wanted_place = lax.div(grid_of((shards * 8, lanes), 1), QT) * 8
+
+    def spread(r):
+        return lax.dot_general(
+            table,
+            jnp.where(place == wanted_place + r, 1.0, 0.0),
+            (((0,), (0,)), ((), ())),
+            precision=HIGH,
+            preferred_element_type=f32,
+        )[:enc_count]
+
+    count = spread(0)
+    wanted = spread(1)
+    total = totals[...]
+    same = lax.div(grid_of((lanes, lanes), 0), QT) == lax.div(grid_of((lanes, lanes), 1), QT)
+    scores = jnp.dot(
+        jnp.log(total),
+        jnp.where(same, token_temp / QT, 0.0),
+        precision=HIGH,
+        preferred_element_type=f32,
+    )
+    raised = jnp.exp(scores / list_temp) * count
+    gather = jnp.where(grid_of((lanes, EMB), 0) == grid_of((lanes, EMB), 1) * QT, 1.0, 0.0)
+    norms[me] = jnp.dot(
+        jnp.broadcast_to(jnp.sum(raised, axis=0, keepdims=True), (8, lanes)),
+        gather,
+        precision=HIGH,
+        preferred_element_type=f32,
+    )
+    second = []
+    for t in range(1, shards):
+        peer = lax.rem(me + t, shards)
+        second.append(remote(norms.at[me], norms.at[me], norm_send.at[t], norm_recv.at[t], peer))
+    for copy in second:
+        copy.start()
+    for copy in second:
+        copy.wait_recv()
+    back = jnp.where(grid_of((EMB, lanes), 0) == lax.div(grid_of((EMB, lanes), 1), QT), 1.0, 0.0)
+    norm = jnp.dot(
+        jnp.sum(norms[...], axis=0), back, precision=HIGH, preferred_element_type=f32
+    )[0:1]
+    score_grad = loss_scale * (raised / norm - wanted) / list_temp
+    totals[...] = (score_grad / QT) / total
+
+    def backward(b, carry):
+        rows = pl.ds(pl.multiple_of(b * block, block), block)
+        some = pl.ds(pl.multiple_of(b * docs, docs), docs)
+        grads = weights[rows].reshape(docs, doc_tokens, lanes) * totals[some][:, None, :]
+        narrow = grads.reshape(block, lanes).astype(bf16)
+        token_narrow[rows] = narrow
+        doc_grad = jnp.dot(narrow, every, preferred_element_type=f32) * inv_root
+        values = unit[rows]
+        proj_grad = factor[rows] * (
+            doc_grad - values * jnp.mean(values * doc_grad, axis=-1, keepdims=True)
+        )
+        narrow_ref[rows] = proj_grad.astype(bf16)
+        narrow_t[b] = jnp.transpose(proj_grad).astype(bf16)
+        return carry
+
+    lax.fori_loop(0, blocks, backward, 0)
+
+    def weight_part(c):
+        columns = pl.ds(pl.multiple_of(c * chunk, chunk), chunk)
+        total = jnp.zeros((EMB, chunk), f32)
+        for b in range(blocks):
+            total = total + jnp.dot(
+                narrow_t[b], hidden[b * block : (b + 1) * block, columns],
+                preferred_element_type=f32,
+            )
+        return total
+
+    pairs = [
+        remote(pair_out.at[t], pair_in.at[t], pair_send.at[t], pair_recv.at[t], mate)
+        for t in range(chips)
+    ]
+    across = []
+    for t in range(chips + 1):
+        if t < chips:
+            there = lax.rem(chip + 1 + t, chips)
+            pair_out[t] = weight_part(there * 2 + (1 - core)).astype(bf16)
+            pairs[t].start()
+        if t > 0:
+            s = t - 1
+            there = lax.rem(chip + 1 + s, chips)
+            part = weight_part(there * 2 + core)
+            pairs[s].wait_recv()
+            part = part + pair_in[s].astype(f32)
+            if s < chips - 1:
+                chip_out[s] = part.astype(bf16)
+                copy = remote(
+                    chip_out.at[s],
+                    chip_in.at[s],
+                    chip_send.at[s],
+                    chip_recv.at[s],
+                    there * 2 + core,
+                )
+                copy.start()
+                across.append(copy)
+            else:
+                own_sum[...] = part
+
+    def query_part(b, sums):
+        rows = pl.ds(pl.multiple_of(b * block, block), block)
+        return sums + lax.dot_general(
+            token_narrow[rows],
+            doc_narrow[rows],
+            (((0,), (0,)), ((), ())),
+            preferred_element_type=f32,
+        )
+
+    sums = lax.fori_loop(0, blocks, query_part, jnp.zeros((lanes, EMB), f32))
+    part_out[...] = sums.reshape(shards, QT, EMB)
+    third = []
+    for t in range(1, shards):
+        peer = lax.rem(me + t, shards)
+        third.append(
+            remote(part_out.at[peer], part_in.at[t], part_send.at[t], part_recv.at[t], peer)
+        )
+    for copy in third:
+        copy.start()
+
+    for copy in across:
+        copy.wait_recv()
+    reduced = own_sum[...]
+    for s in range(chips - 1):
+        reduced = reduced + chip_in[s].astype(f32)
+    own_rows = pl.ds(pl.multiple_of(me * chunk, chunk), chunk)
+    gathered_ref[own_rows] = jnp.transpose(reduced * (1.0 / (enc_count * shards))).astype(bf16)
+
+    ring = []
+    for s in range(chips - 1):
+        there = lax.rem(chip + 1 + s, chips)
+        ring.append(
+            remote(
+                gathered_ref.at[own_rows],
+                gathered_ref.at[own_rows],
+                ring_send.at[s],
+                ring_recv.at[s],
+                there * 2 + core,
+            )
+        )
+    for copy in ring:
+        copy.start()
+    to_mate = [
+        remote(
+            gathered_ref.at[own_rows],
+            gathered_ref.at[own_rows],
+            mate_send.at[chips - 1],
+            mate_recv.at[chips - 1],
+            mate,
+        )
+    ]
+    to_mate[0].start()
+
+    for copy in third:
+        copy.wait_recv()
+    query_sum = part_out[me]
+    for t in range(1, shards):
+        query_sum = query_sum + part_in[t]
+    query_sum = query_sum * inv_root
+    query_grad_ref[...] = query_factor * (
+        query_sum - query_unit * jnp.mean(query_unit * query_sum, axis=-1, keepdims=True)
+    )
+
+    for s in range(chips - 1):
+        ring[s].wait_recv()
+        source = lax.rem(chip + 2 * chips - 1 - s, chips) * 2 + core
+        rows = pl.ds(pl.multiple_of(source * chunk, chunk), chunk)
+        copy = remote(
+            gathered_ref.at[rows], gathered_ref.at[rows], mate_send.at[s], mate_recv.at[s], mate
+        )
+        copy.start()
+        to_mate.append(copy)
+    for copy in to_mate:
+        copy.wait_recv()
+    for copy in first + second + third + pairs + across + ring + to_mate:
+        copy.wait_send()
+
+
+def exchange(flat_hidden, proj_weight, query, lists, lengths, shards, enc_count, doc_tokens):
+    tokens, hid = flat_hidden.shape
+    lanes = shards * QT
+    docs = 8
+    block = docs * doc_tokens
+    blocks = tokens // block
+    chunk = hid // shards
+    chips = shards // 2
+    f32, bf16 = jnp.float32, jnp.bfloat16
+    in_vmem = pl.BlockSpec(memory_space=pltpu.VMEM)
+    in_hbm = pl.BlockSpec(memory_space=pl.ANY)
+    dma = pltpu.SemaphoreType.DMA
+    return pl.pallas_call(
+        functools.partial(exchange_kernel, shards, enc_count, doc_tokens),
+        out_shape=(
+            jax.ShapeDtypeStruct((tokens, EMB), bf16),
+            jax.ShapeDtypeStruct((hid, EMB), bf16),
+            jax.ShapeDtypeStruct((QT, EMB), f32),
+        ),
+        in_specs=[in_hbm, in_hbm, in_vmem, in_vmem, in_vmem],
+        out_specs=(in_vmem, in_vmem, in_vmem),
+        scratch_shapes=[
+            pltpu.VMEM((tokens, hid), bf16),
+            pltpu.VMEM((hid, EMB), bf16),
+            pltpu.VMEM((tokens, EMB), f32),
+            pltpu.VMEM((tokens, EMB), f32),
+            pltpu.VMEM((tokens, EMB), bf16),
+            pltpu.VMEM((tokens, lanes), f32),
+            pltpu.VMEM((enc_count, lanes), f32),
+            pltpu.VMEM((tokens, lanes), bf16),
+            pltpu.VMEM((blocks, EMB, block), bf16),
+            pltpu.VMEM((shards, QT, EMB), bf16),
+            pltpu.VMEM((shards, 8, EMB), f32),
+            pltpu.VMEM((shards, 8, EMB), f32),
+            pltpu.VMEM((shards, 8, EMB), f32),
+            pltpu.VMEM((shards, QT, EMB), f32),
+            pltpu.VMEM((shards, QT, EMB), f32),
+            pltpu.VMEM((chips, EMB, chunk), bf16),
+            pltpu.VMEM((chips, EMB, chunk), bf16),
+            pltpu.VMEM((chips, EMB, chunk), bf16),
+            pltpu.VMEM((chips, EMB, chunk), bf16),
+            pltpu.VMEM((EMB, chunk), f32),
+            dma((blocks + 1,)),
+        ]
+        + [dma((shards,))] * 8
+        + [dma((chips,))] * 8,
+        compiler_params=pltpu.CompilerParams(
+            collective_id=0, has_side_effects=True, vmem_limit_bytes=48 * 1024 * 1024
+        ),
+    )(flat_hidden, proj_weight, query, lists, lengths)
+
+
+def spread_kernel(narrow_ref, weight_ref, gathered_ref, hidden_grad_ref, weight_grad_ref):
+    hidden_grad_ref[...] = lax.dot_general(
+        narrow_ref[...],
+        weight_ref[...],
+        (((1,), (1,)), ((), ())),
+        preferred_element_type=jnp.float32,
+    ).astype(jnp.bfloat16)
+    weight_grad_ref[...] = gathered_ref[...].astype(jnp.float32)
+
+
+def hidden_gradient(proj_narrow, proj_weight, gathered, steps=8):
+    tokens = proj_narrow.shape[0]
+    hid = proj_weight.shape[0]
+    return pl.pallas_call(
+        spread_kernel,
+        grid=(steps,),
+        out_shape=(
+            jax.ShapeDtypeStruct((tokens, hid), jnp.bfloat16),
+            jax.ShapeDtypeStruct((hid, EMB), jnp.float32),
+        ),
+        in_specs=[
+            pl.BlockSpec((tokens // steps, EMB), lambda i: (i, 0)),
+            pl.BlockSpec((hid, EMB), lambda i: (0, 0)),
+            pl.BlockSpec((hid // steps, EMB), lambda i: (i, 0)),
+        ],
+        out_specs=(
+            pl.BlockSpec((tokens // steps, hid), lambda i: (i, 0)),
+            pl.BlockSpec((hid // steps, EMB), lambda i: (i, 0)),
+        ),
+        compiler_params=pltpu.CompilerParams(vmem_limit_bytes=48 * 1024 * 1024),
+    )(proj_narrow, proj_weight, gathered)
+
+
+def with_kernels(
+    doc_hidden, proj_weight, query_reps, teacher, cand_peer, cand_doc, tile_count, doc_len
+):
+    enc_count, doc_tokens, hidden_part = doc_hidden.shape
+    shards = lax.axis_size("dp")
+    me = lax.axis_index("dp")
+    slots = cand_doc.shape[1]
+    valid = (jnp.arange(slots)[None, :] // TILE < tile_count[:, None]).astype(jnp.float32)
+    ident = (cand_peer[:, :, 0] * EMB + cand_doc).astype(jnp.float32)
+    lists = jnp.concatenate(
+        [teacher, valid, ident, jnp.zeros((5, slots), jnp.float32)], axis=0
+    )
+    own_len = lax.dynamic_slice_in_dim(doc_len, me * enc_count, enc_count).astype(jnp.float32)
+    lengths = jnp.broadcast_to(own_len[:, None], (enc_count, shards * QT))
+    proj_narrow, gathered, grad_query = exchange(
+        doc_hidden.reshape(enc_count * doc_tokens, hidden_part),
+        proj_weight,
+        query_reps.reshape(QT, EMB),
+        lists,
+        lengths,
+        shards,
+        enc_count,
+        doc_tokens,
+    )
+    grad_hidden, grad_weight = hidden_gradient(proj_narrow, proj_weight, gathered)
+    return (
+        grad_hidden.reshape(enc_count, doc_tokens, hidden_part),
+        grad_weight,
+        grad_query.reshape(1, QT, EMB),
+    )
+
+
 def solution(mesh):
+    plain = mesh.shape["tensor"] > 1 or mesh.shape["dp"] % 2 > 0
     placed = (
         P(("groups", "dp"), None, "tensor"),
         P("tensor", None),
@@ -104,7 +573,7 @@
         P("groups"),
     )
     return jax.shard_map(
-        with_collectives,
+        with_collectives if plain else with_kernels,
         mesh=mesh,
         in_specs=placed,
         out_specs=(

time: 270 us -> 68 us (0.25)
  waiting for transfers between devices: 135 us -> 0 us
  blocking collectives: 70 us -> 0 us
  Pallas kernels: 0 us -> 60.9 us
  matrix products: 28.9 us -> 0 us
  between operations: 14.9 us -> 1.3 us
  other arithmetic: 14.4 us -> 2.22 us
    psum x1 -> x0, waiting for transfers between devices: 99.8 us -> none  [with_collectives(): grad_weight = lax.psum(weight_part, 'dp') / (enc_count * shards)]
    pallas_call x0 -> x2, Pallas kernels: none -> 60.9 us  [the longest x1 54 us: exchange(): pl.pallas_call(functools.partial(exchange_kernel, shards, enc_count, doc_...]
    all_gather x2 -> x0, blocking collectives: 41 us -> none  [the longest x1 23.2 us: with_collectives(): lax.all_gather(jnp.stack([count, wanted], axis=1), 'dp', axis=0, tiled=True)]
    reduce_scatter x1 -> x0, waiting for transfers between devices: 35.2 us -> none  [with_collectives(): lax.psum_scatter(query_part, 'dp', scatter_dimension=0, tiled=True)]
    psum x1 -> x0, blocking collectives: 29 us -> none  [with_collectives(): norm = lax.psum(jnp.sum(raised, axis=-1), 'dp')]
    dot_general x6 -> x0, matrix products: 28.9 us -> none  [the longest x1 6.93 us: with_collectives(): lax.dot_general(flat_hidden, proj_narrow, (((0,), (0,)), ((), ())), prefe...]
    convert_element_type x6 -> x3, other arithmetic: 5.98 us -> 1.47 us  [the longest x1 0.76 us: with_kernels(): lax.dynamic_slice_in_dim(doc_len, me * enc_count, enc_count)]
    reduce_sum x7 -> x0, other arithmetic: 3.82 us -> none  [the longest x1 1.29 us: list_tables(): target = target / jnp.sum(target, axis=-1, keepdims=True)]
  transfers between devices with their start and end apart: 2 -> 0, of which waited for: 2 -> 0; matrix products, arithmetic and copies ran while one was open for 7% -> 0% of each run, Pallas kernels for 0% -> 0%
where the time goes in v2:
time: 68 us; the launch traced here: 67 us
  Pallas kernels  60.9 us (90%)
  local copies, waits for them, and re-layouts  2.68 us (4%)
  other arithmetic  2.22 us (3%)
  between operations  1.3 us (2%)
    pallas_call x1, Pallas kernels, exchange(): pl.pallas_call(functools.partial(exchange_kernel, shards, enc_count, doc_...  54 us
    pallas_call x1, Pallas kernels, hidden_gradient(): pl.pallas_call(spread_kernel, grid=(steps,), out_shape=(jax.ShapeDtypeStr...  6.88 us
    unnamed x5, local copies, waits for them, and re-layouts  2.53 us

profile of v2, /device:TPU:1, one launch (start us, length us, event | category | flops | bytes accessed | tf_op | source)
XLA Modules:
  0.0 67.0 jit_solution(10680551895987052078)
XLA Ops:
  1.3 0.8 %dynamic-slice_convert_fusion = f32[40]{0:T(128)S(1)} fusion(s32[640]{0:T(1024)} %param.15, s32[]{:T(128)S(6)} %select_n.17), kind=kLoop, calls=%fused_computation.8 | loop fusion | flops 40 | bytes 324 | tf_op jit(solution)/shard_map/convert_element_type | solution.py:543
  2.1 0.1 pad.3.clone
  2.1 0.7 %fusion = f32[1,256]{1,0:T(1,128)S(1)} fusion(s32[1,256]{1,0:T(1,128)} %param.13, s32[1,256,1]{1,2,0:T(1,128)} %param.12), kind=kLoop, calls=%fused_computation.7 | loop fusion | flops 768 | bytes 3072 | tf_op jit(solution)/shard_map/convert_element_type | solution.py:539
  2.8 0.7 %maximum_maximum_fusion.list_ref = f32[8,256]{1,0:T(8,128)S(1)} fusion(f32[1,256]{1,0:T(1,128)S(1)} %fusion, f32[1,256]{1,0:T(1,128)S(1)} %compare_convert_fusion, f32[1,256]{1,0:T(1,128)} %param.11, f32[8]{0:T(128)S(1)} %pad.3.clone), kind=kLoop, calls=%fused_computation | loop fusion | flops 6144 | bytes 11296 | tf_op jit(solution)/shard_map/concatenate | solution.py:540
  3.6 0.1 broadcast_in_dim.5.length_ref
  3.7 0.0 copy-start
  3.7 1.2 %copy-done = bf16[4096,128]{1,0:T(8,128)(2,1)S(1)} copy-done((bf16[4096,128]{1,0:T(8,128)(2,1)S(1)}, bf16[4096,128]{1,0:T(8,128)(2,1)}, u32[]{:S(2)}) %copy-start) | copy-done | bytes 1048600
  4.9 0.0 copy-start.1
  4.9 0.7 %copy-done.1 = bf16[1,32,128]{2,1,0:T(8,128)(2,1)S(1)} copy-done((bf16[1,32,128]{2,1,0:T(8,128)(2,1)S(1)}, bf16[1,32,128]{2,1,0:T(8,128)(2,1)}, u32[]{:S(2)}) %copy-start.1) | copy-done | bytes 8216
  5.6 54.0 %shard_map.103 = (bf16[1280,128]{1,0:T(8,128)(2,1)S(1)}, bf16[4096,128]{1,0:T(8,128)(2,1)S(1)}, f32[32,128]{1,0:T(8,128)S(1)}) custom-call(bf16[1280,4096]{1,0:T(8,128)(2,1)} %bitcast.12, bf16[4096,128]{1,0:T(8,128)(2,1)S(1)} %copy-done, bf16[32,128]{1,0:T(8,128)(2,1)S(1)} %bitcast.11, f32[8,256]{1,0:T(8,128)S(1)} %maximum_maximum_fusion.list_ref, ...), custom_call_target="tpu_custom_call" | custom-call | tf_op jit(solution)/shard_map/pallas_call | solution.py:458
  59.6 6.9 %shard_map.104 = (bf16[1280,4096]{1,0:T(8,128)(2,1)}, f32[4096,128]{1,0:T(8,128)}) custom-call(bf16[1280,128]{1,0:T(8,128)(2,1)S(1)} %get-tuple-element.8.narrow_ref, bf16[4096,128]{1,0:T(8,128)(2,1)S(1)} %copy-done, bf16[4096,128]{1,0:T(8,128)(2,1)S(1)} %get-tuple-element.9.gathered_ref), custom_call_target="tpu_custom_call" | custom-call | tf_op jit(solution)/shard_map/pallas_call | solution.py:511
  66.4 0.6 copy.13
  (2 shorter events, 0.0 us)
Async XLA Ops:
  3.7 1.2 %copy-start = (bf16[4096,128]{1,0:T(8,128)(2,1)S(1)}, bf16[4096,128]{1,0:T(8,128)(2,1)}, u32[]{:S(2)}) copy-start(bf16[4096,128]{1,0:T(8,128)(2,1)} %weight_ref.1) | copy-start | bytes 3145732
  4.9 0.7 %copy-start.1 = (bf16[1,32,128]{2,1,0:T(8,128)(2,1)S(1)}, bf16[1,32,128]{2,1,0:T(8,128)(2,1)}, u32[]{:S(2)}) copy-start(bf16[1,32,128]{2,1,0:T(8,128)(2,1)} %param.10) | copy-start | bytes 24580

commit v3 on v2

--- a/solution.py
+++ b/solution.py
@@ -115,6 +115,7 @@
     narrow_ref,
     gathered_ref,
     query_grad_ref,
+    weight_t_ref,
     hidden,
     weight,
     unit,
@@ -134,6 +135,8 @@
     pair_in,
     chip_out,
     chip_in,
+    side_out,
+    side_in,
     own_sum,
     load_sem,
     query_send,
@@ -152,6 +155,10 @@
     ring_recv,
     mate_send,
     mate_recv,
+    side_send,
+    side_recv,
+    fan_send,
+    fan_recv,
 ):
     f32, bf16 = jnp.float32, jnp.bfloat16
     me = lax.axis_index("dp")
@@ -159,6 +166,13 @@
     chip = lax.div(me, 2)
     chips = shards // 2
     mate = chip * 2 + (1 - core)
+    lines = chips // 2
+    line, side = lax.div(chip, 2), lax.rem(chip, 2)
+    beside = (line * 2 + 1 - side) * 2 + core
+
+    def shard_at(line_at, side_at, core_at):
+        return (line_at * 2 + side_at) * 2 + core_at
+
     inv_root = 1.0 / math.sqrt(EMB)
     tokens, hid = hidden.shape
     lanes = shards * QT
@@ -203,14 +217,22 @@
     target = target / jnp.sum(target, axis=-1, keepdims=True)
     ident = list_ref[2:3, :]
     row = grid_of((8, slots), 0)
-    terms = jnp.where(row == 0, valid, jnp.where(row == 1, target, 0.0))
+    high = target.astype(bf16).astype(f32)
+    middle = (target - high).astype(bf16).astype(f32)
+    low = target - high - middle
+    terms = jnp.where(
+        row == 0,
+        valid,
+        jnp.where(
+            row == 1, high, jnp.where(row == 2, middle, jnp.where(row == 3, low, 0.0))
+        ),
+    ).astype(bf16)
     for p in range(shards):
         named = (grid_of((EMB, slots), 0) + p * EMB).astype(f32) == ident
         table_out[p] = lax.dot_general(
             terms,
-            jnp.where(named, 1.0, 0.0),
+            jnp.where(named, 1.0, 0.0).astype(bf16),
             (((1,), (1,)), ((), ())),
-            precision=HIGH,
             preferred_element_type=f32,
         )
     table_in[me] = table_out[me]
@@ -266,17 +288,17 @@
     place = grid_of((shards * 8, lanes), 0)
     wanted_place = lax.div(grid_of((shards * 8, lanes), 1), QT) * 8
 
-    def spread(r):
+    def spread(r, last):
         return lax.dot_general(
             table,
-            jnp.where(place == wanted_place + r, 1.0, 0.0),
+            jnp.where((place >= wanted_place + r) & (place <= wanted_place + last), 1.0, 0.0),
             (((0,), (0,)), ((), ())),
             precision=HIGH,
             preferred_element_type=f32,
         )[:enc_count]
 
-    count = spread(0)
-    wanted = spread(1)
+    count = spread(0, 0)
+    wanted = spread(1, 3)
     total = totals[...]
     same = lax.div(grid_of((lanes, lanes), 0), QT) == lax.div(grid_of((lanes, lanes), 1), QT)
     scores = jnp.dot(
@@ -340,30 +362,46 @@
         for t in range(chips)
     ]
     across = []
+    sides = [
+        remote(side_out.at[t], side_in.at[t], side_send.at[t], side_recv.at[t], beside)
+        for t in range(lines)
+    ]
+
+    def bound_for(t):
+        there = lax.rem(line + 1 + t % lines, lines)
+        return there, (1 - side if t < lines else side)
+
     for t in range(chips + 1):
         if t < chips:
-            there = lax.rem(chip + 1 + t, chips)
-            pair_out[t] = weight_part(there * 2 + (1 - core)).astype(bf16)
+            there, at = bound_for(t)
+            pair_out[t] = weight_part(shard_at(there, at, 1 - core)).astype(bf16)
             pairs[t].start()
         if t > 0:
             s = t - 1
-            there = lax.rem(chip + 1 + s, chips)
-            part = weight_part(there * 2 + core)
+            there, at = bound_for(s)
+            part = weight_part(shard_at(there, at, core))
             pairs[s].wait_recv()
             part = part + pair_in[s].astype(f32)
-            if s < chips - 1:
-                chip_out[s] = part.astype(bf16)
-                copy = remote(
-                    chip_out.at[s],
-                    chip_in.at[s],
-                    chip_send.at[s],
-                    chip_recv.at[s],
-                    there * 2 + core,
-                )
-                copy.start()
-                across.append(copy)
+            if s < lines:
+                side_out[s] = part.astype(bf16)
+                sides[s].start()
             else:
-                own_sum[...] = part
+                k = s - lines
+                sides[k].wait_recv()
+                part = part + side_in[k].astype(f32)
+                if k < lines - 1:
+                    chip_out[k] = part.astype(bf16)
+                    copy = remote(
+                        chip_out.at[k],
+                        chip_in.at[k],
+                        chip_send.at[k],
+                        chip_recv.at[k],
+                        shard_at(there, side, core),
+                    )
+                    copy.start()
+                    across.append(copy)
+                else:
+                    own_sum[...] = part
 
     def query_part(b, sums):
         rows = pl.ds(pl.multiple_of(b * block, block), block)
@@ -385,38 +423,33 @@
     for copy in third:
         copy.start()
 
+    for p in range(shards):
+        weight_t_ref[:, p * chunk : (p + 1) * chunk] = jnp.transpose(
+            weight[p * chunk : (p + 1) * chunk]
+        )
+
     for copy in across:
         copy.wait_recv()
     reduced = own_sum[...]
-    for s in range(chips - 1):
+    for s in range(lines - 1):
         reduced = reduced + chip_in[s].astype(f32)
     own_rows = pl.ds(pl.multiple_of(me * chunk, chunk), chunk)
     gathered_ref[own_rows] = jnp.transpose(reduced * (1.0 / (enc_count * shards))).astype(bf16)
 
+    def pass_on(source, send, recv, peer):
+        rows = pl.ds(pl.multiple_of(source * chunk, chunk), chunk)
+        copy = remote(gathered_ref.at[rows], gathered_ref.at[rows], send, recv, peer)
+        copy.start()
+        return copy
+
     ring = []
-    for s in range(chips - 1):
-        there = lax.rem(chip + 1 + s, chips)
+    for s in range(lines - 1):
+        there = lax.rem(line + 1 + s, lines)
         ring.append(
-            remote(
-                gathered_ref.at[own_rows],
-                gathered_ref.at[own_rows],
-                ring_send.at[s],
-                ring_recv.at[s],
-                there * 2 + core,
-            )
-        )
-    for copy in ring:
-        copy.start()
-    to_mate = [
-        remote(
-            gathered_ref.at[own_rows],
-            gathered_ref.at[own_rows],
-            mate_send.at[chips - 1],
-            mate_recv.at[chips - 1],
-            mate,
-        )
-    ]
-    to_mate[0].start()
+            pass_on(me, ring_send.at[s], ring_recv.at[s], shard_at(there, side, core))
+        )
+    fan = [pass_on(me, fan_send.at[lines - 1], fan_recv.at[lines - 1], beside)]
+    to_mate = [pass_on(me, mate_send.at[lines - 1], mate_recv.at[lines - 1], mate)]
 
     for copy in third:
         copy.wait_recv()
@@ -428,18 +461,29 @@
         query_sum - query_unit * jnp.mean(query_unit * query_sum, axis=-1, keepdims=True)
     )
 
-    for s in range(chips - 1):
+    def from_beside(slot, line_at):
+        fan[0 if slot == lines - 1 else slot + 1].wait_recv()
+        to_mate.append(
+            pass_on(
+                shard_at(line_at, 1 - side, core),
+                mate_send.at[lines + slot],
+                mate_recv.at[lines + slot],
+                mate,
+            )
+        )
+
+    from_beside(lines - 1, line)
+    sources = [lax.rem(line + 2 * lines - 1 - s, lines) for s in range(lines - 1)]
+    for s in range(lines - 1):
         ring[s].wait_recv()
-        source = lax.rem(chip + 2 * chips - 1 - s, chips) * 2 + core
-        rows = pl.ds(pl.multiple_of(source * chunk, chunk), chunk)
-        copy = remote(
-            gathered_ref.at[rows], gathered_ref.at[rows], mate_send.at[s], mate_recv.at[s], mate
-        )
-        copy.start()
-        to_mate.append(copy)
+        source = shard_at(sources[s], side, core)
+        fan.append(pass_on(source, fan_send.at[s], fan_recv.at[s], beside))
+        to_mate.append(pass_on(source, mate_send.at[s], mate_recv.at[s], mate))
+    for s in range(lines - 1):
+        from_beside(s, sources[s])
     for copy in to_mate:
         copy.wait_recv()
-    for copy in first + second + third + pairs + across + ring + to_mate:
+    for copy in first + second + third + pairs + sides + across + ring + fan + to_mate:
         copy.wait_send()
 
 
@@ -453,7 +497,7 @@
     chips = shards // 2
     f32, bf16 = jnp.float32, jnp.bfloat16
     in_vmem = pl.BlockSpec(memory_space=pltpu.VMEM)
-    in_hbm = pl.BlockSpec(memory_space=pl.ANY)
+    in_hbm = pl.BlockSpec(memory_space=pltpu.HBM)
     dma = pltpu.SemaphoreType.DMA
     return pl.pallas_call(
         functools.partial(exchange_kernel, shards, enc_count, doc_tokens),
@@ -461,9 +505,10 @@
             jax.ShapeDtypeStruct((tokens, EMB), bf16),
             jax.ShapeDtypeStruct((hid, EMB), bf16),
             jax.ShapeDtypeStruct((QT, EMB), f32),
+            jax.ShapeDtypeStruct((EMB, hid), bf16),
         ),
         in_specs=[in_hbm, in_hbm, in_vmem, in_vmem, in_vmem],
-        out_specs=(in_vmem, in_vmem, in_vmem),
+        out_specs=(in_vmem, in_vmem, in_vmem, in_vmem),
         scratch_shapes=[
             pltpu.VMEM((tokens, hid), bf16),
             pltpu.VMEM((hid, EMB), bf16),
@@ -484,30 +529,29 @@
             pltpu.VMEM((chips, EMB, chunk), bf16),
             pltpu.VMEM((chips, EMB, chunk), bf16),
             pltpu.VMEM((chips, EMB, chunk), bf16),
+            pltpu.VMEM((chips // 2, EMB, chunk), bf16),
+            pltpu.VMEM((chips // 2, EMB, chunk), bf16),
             pltpu.VMEM((EMB, chunk), f32),
             dma((blocks + 1,)),
         ]
         + [dma((shards,))] * 8
-        + [dma((chips,))] * 8,
+        + [dma((chips,))] * 12,
         compiler_params=pltpu.CompilerParams(
             collective_id=0, has_side_effects=True, vmem_limit_bytes=48 * 1024 * 1024
         ),
     )(flat_hidden, proj_weight, query, lists, lengths)
 
 
-def spread_kernel(narrow_ref, weight_ref, gathered_ref, hidden_grad_ref, weight_grad_ref):
-    hidden_grad_ref[...] = lax.dot_general(
-        narrow_ref[...],
-        weight_ref[...],
-        (((1,), (1,)), ((), ())),
-        preferred_element_type=jnp.float32,
+def spread_kernel(narrow_ref, weight_t_ref, gathered_ref, hidden_grad_ref, weight_grad_ref):
+    hidden_grad_ref[...] = jnp.dot(
+        narrow_ref[...], weight_t_ref[...], preferred_element_type=jnp.float32
     ).astype(jnp.bfloat16)
     weight_grad_ref[...] = gathered_ref[...].astype(jnp.float32)
 
 
-def hidden_gradient(proj_narrow, proj_weight, gathered, steps=8):
+def hidden_gradient(proj_narrow, weight_t, gathered, steps=8):
     tokens = proj_narrow.shape[0]
-    hid = proj_weight.shape[0]
+    hid = weight_t.shape[1]
     return pl.pallas_call(
         spread_kernel,
         grid=(steps,),
@@ -517,7 +561,7 @@
         ),
         in_specs=[
             pl.BlockSpec((tokens // steps, EMB), lambda i: (i, 0)),
-            pl.BlockSpec((hid, EMB), lambda i: (0, 0)),
+            pl.BlockSpec((EMB, hid), lambda i: (0, 0)),
             pl.BlockSpec((hid // steps, EMB), lambda i: (i, 0)),
         ],
         out_specs=(
@@ -525,7 +569,7 @@
             pl.BlockSpec((hid // steps, EMB), lambda i: (i, 0)),
         ),
         compiler_params=pltpu.CompilerParams(vmem_limit_bytes=48 * 1024 * 1024),
-    )(proj_narrow, proj_weight, gathered)
+    )(proj_narrow, weight_t, gathered)
 
 
 def with_kernels(
@@ -542,7 +586,7 @@
     )
     own_len = lax.dynamic_slice_in_dim(doc_len, me * enc_count, enc_count).astype(jnp.float32)
     lengths = jnp.broadcast_to(own_len[:, None], (enc_count, shards * QT))
-    proj_narrow, gathered, grad_query = exchange(
+    proj_narrow, gathered, grad_query, weight_t = exchange(
         doc_hidden.reshape(enc_count * doc_tokens, hidden_part),
         proj_weight,
         query_reps.reshape(QT, EMB),
@@ -552,7 +596,7 @@
         enc_count,
         doc_tokens,
     )
-    grad_hidden, grad_weight = hidden_gradient(proj_narrow, proj_weight, gathered)
+    grad_hidden, grad_weight = hidden_gradient(proj_narrow, weight_t, gathered)
     return (
         grad_hidden.reshape(enc_count, doc_tokens, hidden_part),
         grad_weight,
@@ -561,7 +605,7 @@
 
 
 def solution(mesh):
-    plain = mesh.shape["tensor"] > 1 or mesh.shape["dp"] % 2 > 0
+    plain = mesh.shape["tensor"] > 1 or mesh.shape["dp"] % 4 > 0
     placed = (
         P(("groups", "dp"), None, "tensor"),
         P("tensor", None),

time: 68 us -> 64.9 us (0.954)
  Pallas kernels: 60.9 us -> 58.4 us
    pallas_call x1, Pallas kernels: 54 us -> 51.6 us  [exchange(): pl.pallas_call(functools.partial(exchange_kernel, shards, enc_count, doc_...]
where the time goes in v3:
time: 64.9 us; the launch traced here: 64.6 us
  Pallas kernels  58.4 us (90%)
  local copies, waits for them, and re-layouts  2.68 us (4%)
  other arithmetic  2.22 us (3%)
  between operations  1.3 us (2%)
    pallas_call x1, Pallas kernels, exchange(): pl.pallas_call(functools.partial(exchange_kernel, shards, enc_count, doc_...  51.6 us
    pallas_call x1, Pallas kernels, hidden_gradient(): pl.pallas_call(spread_kernel, grid=(steps,), out_shape=(jax.ShapeDtypeStr...  6.81 us
    unnamed x5, local copies, waits for them, and re-layouts  2.53 us

profile of v3, /device:TPU:1, one launch (start us, length us, event | category | flops | bytes accessed | tf_op | source)
XLA Modules:
  0.0 64.6 jit_solution(3412241361370285188)
XLA Ops:
  1.3 0.8 %dynamic-slice_convert_fusion = f32[40]{0:T(128)S(1)} fusion(s32[640]{0:T(1024)} %param.15, s32[]{:T(128)S(6)} %select_n.17), kind=kLoop, calls=%fused_computation.8 | loop fusion | flops 40 | bytes 324 | tf_op jit(solution)/shard_map/convert_element_type | solution.py:587
  2.1 0.1 pad.3.clone
  2.1 0.7 %fusion = f32[1,256]{1,0:T(1,128)S(1)} fusion(s32[1,256]{1,0:T(1,128)} %param.13, s32[1,256,1]{1,2,0:T(1,128)} %param.12), kind=kLoop, calls=%fused_computation.7 | loop fusion | flops 768 | bytes 3072 | tf_op jit(solution)/shard_map/convert_element_type | solution.py:583
  2.8 0.7 %maximum_maximum_fusion.list_ref = f32[8,256]{1,0:T(8,128)S(1)} fusion(f32[1,256]{1,0:T(1,128)S(1)} %fusion, f32[1,256]{1,0:T(1,128)S(1)} %compare_convert_fusion, f32[1,256]{1,0:T(1,128)} %param.11, f32[8]{0:T(128)S(1)} %pad.3.clone), kind=kLoop, calls=%fused_computation | loop fusion | flops 6144 | bytes 11296 | tf_op jit(solution)/shard_map/concatenate | solution.py:584
  3.6 0.1 broadcast_in_dim.5.length_ref
  3.7 0.0 copy-start
  3.7 1.2 %copy-done = bf16[4096,128]{1,0:T(8,128)(2,1)S(1)} copy-done((bf16[4096,128]{1,0:T(8,128)(2,1)S(1)}, bf16[4096,128]{1,0:T(8,128)(2,1)}, u32[]{:S(2)}) %copy-start) | copy-done | bytes 1048600
  4.9 0.0 copy-start.1
  4.9 0.7 %copy-done.1 = bf16[1,32,128]{2,1,0:T(8,128)(2,1)S(1)} copy-done((bf16[1,32,128]{2,1,0:T(8,128)(2,1)S(1)}, bf16[1,32,128]{2,1,0:T(8,128)(2,1)}, u32[]{:S(2)}) %copy-start.1) | copy-done | bytes 8216
  5.6 51.6 %shard_map.103 = (bf16[1280,128]{1,0:T(8,128)(2,1)S(1)}, bf16[4096,128]{1,0:T(8,128)(2,1)S(1)}, f32[32,128]{1,0:T(8,128)S(1)}, bf16[128,4096]{1,0:T(8,128)(2,1)S(1)}) custom-call(bf16[1280,4096]{1,0:T(8,128)(2,1)} %bitcast.12, bf16[4096,128]{1,0:T(8,128)(2,1)S(1)} %copy-done, bf16[32,128]{1,0:T(8,128)(2,1)S(1)} %bitcast.11, ...), custom_call_target="tpu_custom_call" | custom-call | tf_op jit(solution)/shard_map/pallas_call | solution.py:502
  57.2 6.8 %shard_map.104 = (bf16[1280,4096]{1,0:T(8,128)(2,1)}, f32[4096,128]{1,0:T(8,128)}) custom-call(bf16[1280,128]{1,0:T(8,128)(2,1)S(1)} %get-tuple-element.9.narrow_ref, bf16[128,4096]{1,0:T(8,128)(2,1)S(1)} %get-tuple-element.10.weight_t_ref, bf16[4096,128]{1,0:T(8,128)(2,1)S(1)} %get-tuple-element.11.gathered_ref), custom_call_target="tpu_custom_call" | custom-call | tf_op jit(solution)/shard_map/pallas_call | solution.py:555
  64.0 0.6 copy.13
  (2 shorter events, 0.0 us)
Async XLA Ops:
  3.7 1.2 %copy-start = (bf16[4096,128]{1,0:T(8,128)(2,1)S(1)}, bf16[4096,128]{1,0:T(8,128)(2,1)}, u32[]{:S(2)}) copy-start(bf16[4096,128]{1,0:T(8,128)(2,1)} %weight_hbm.1) | copy-start | bytes 3145732
  4.9 0.7 %copy-start.1 = (bf16[1,32,128]{2,1,0:T(8,128)(2,1)S(1)}, bf16[1,32,128]{2,1,0:T(8,128)(2,1)}, u32[]{:S(2)}) copy-start(bf16[1,32,128]{2,1,0:T(8,128)(2,1)} %param.10) | copy-start | bytes 24580

commit v4 on v3

--- a/solution.py
+++ b/solution.py
@@ -95,6 +95,7 @@
     return (grad_hidden, grad_weight, grad_query)
 
 
+TABLE = 16
 HIGH = lax.Precision.HIGHEST
 MESH = pl.DeviceIdType.MESH
 
@@ -125,7 +126,6 @@
     totals,
     token_narrow,
     narrow_t,
-    queries,
     table_out,
     table_in,
     norms,
@@ -139,8 +139,6 @@
     side_in,
     own_sum,
     load_sem,
-    query_send,
-    query_recv,
     table_send,
     table_recv,
     norm_send,
@@ -210,7 +208,6 @@
     query = query_ref[...].astype(f32)
     query_factor = lax.rsqrt(jnp.mean(query * query, axis=-1, keepdims=True) + epsilon)
     query_unit = query * query_factor
-    queries[me] = query_unit.astype(bf16)
     slots = list_ref.shape[1]
     valid = list_ref[1:2, :]
     target = jnp.exp(list_ref[0:1, :]) * valid
@@ -229,21 +226,33 @@
     ).astype(bf16)
     for p in range(shards):
         named = (grid_of((EMB, slots), 0) + p * EMB).astype(f32) == ident
-        table_out[p] = lax.dot_general(
+        sums = lax.dot_general(
             terms,
             jnp.where(named, 1.0, 0.0).astype(bf16),
             (((1,), (1,)), ((), ())),
             preferred_element_type=f32,
         )
+        listed = sums[0:1]
+        aim = sums[1:2] + sums[2:3] + sums[3:4]
+        high = aim.astype(bf16).astype(f32)
+        middle = (aim - high).astype(bf16).astype(f32)
+        low = aim - high - middle
+        kind = grid_of((TABLE, EMB), 0)
+        table = jnp.where(
+            kind == 0,
+            listed,
+            jnp.where(
+                kind == 1, high, jnp.where(kind == 2, middle, jnp.where(kind == 3, low, 0.0))
+            ),
+        )
+        table_out[p, 0:QT] = query_unit.astype(bf16)
+        table_out[p, QT : QT + TABLE] = table.astype(bf16)
     table_in[me] = table_out[me]
 
     pl.semaphore_wait(barrier, shards - 1)
     first = []
     for t in range(1, shards):
         peer = lax.rem(me + t, shards)
-        first.append(
-            remote(queries.at[me], queries.at[me], query_send.at[t], query_recv.at[t], peer)
-        )
         first.append(
             remote(table_out.at[peer], table_in.at[me], table_send.at[t], table_recv.at[t], peer)
         )
@@ -267,7 +276,7 @@
 
     for copy in first:
         copy.wait_recv()
-    every = queries[...].reshape(lanes, EMB)
+    every = table_in[:, 0:QT].reshape(lanes, EMB)
 
     def score(b, carry):
         rows = pl.ds(pl.multiple_of(b * block, block), block)
@@ -284,16 +293,17 @@
 
     lax.fori_loop(0, blocks, score, 0)
 
-    table = table_in[...].reshape(shards * 8, EMB)
-    place = grid_of((shards * 8, lanes), 0)
-    wanted_place = lax.div(grid_of((shards * 8, lanes), 1), QT) * 8
+    table = table_in[:, QT : QT + TABLE].reshape(shards * TABLE, EMB)
+    place = grid_of((shards * TABLE, lanes), 0)
+    wanted_place = lax.div(grid_of((shards * TABLE, lanes), 1), QT) * TABLE
 
     def spread(r, last):
         return lax.dot_general(
             table,
-            jnp.where((place >= wanted_place + r) & (place <= wanted_place + last), 1.0, 0.0),
+            jnp.where((place >= wanted_place + r) & (place <= wanted_place + last), 1.0, 0.0).astype(
+                bf16
+            ),
             (((0,), (0,)), ((), ())),
-            precision=HIGH,
             preferred_element_type=f32,
         )[:enc_count]
 
@@ -519,9 +529,8 @@
             pltpu.VMEM((enc_count, lanes), f32),
             pltpu.VMEM((tokens, lanes), bf16),
             pltpu.VMEM((blocks, EMB, block), bf16),
-            pltpu.VMEM((shards, QT, EMB), bf16),
-            pltpu.VMEM((shards, 8, EMB), f32),
-            pltpu.VMEM((shards, 8, EMB), f32),
+            pltpu.VMEM((shards, QT + TABLE, EMB), bf16),
+            pltpu.VMEM((shards, QT + TABLE, EMB), bf16),
             pltpu.VMEM((shards, 8, EMB), f32),
             pltpu.VMEM((shards, QT, EMB), f32),
             pltpu.VMEM((shards, QT, EMB), f32),
@@ -534,10 +543,10 @@
             pltpu.VMEM((EMB, chunk), f32),
             dma((blocks + 1,)),
         ]
-        + [dma((shards,))] * 8
+        + [dma((shards,))] * 6
         + [dma((chips,))] * 12,
         compiler_params=pltpu.CompilerParams(
-            collective_id=0, has_side_effects=True, vmem_limit_bytes=48 * 1024 * 1024
+            collective_id=0, has_side_effects=True, vmem_limit_bytes=60 * 1024 * 1024
         ),
     )(flat_hidden, proj_weight, query, lists, lengths)
 
@@ -568,7 +577,7 @@
             pl.BlockSpec((tokens // steps, hid), lambda i: (i, 0)),
             pl.BlockSpec((hid // steps, EMB), lambda i: (i, 0)),
         ),
-        compiler_params=pltpu.CompilerParams(vmem_limit_bytes=48 * 1024 * 1024),
+        compiler_params=pltpu.CompilerParams(vmem_limit_bytes=60 * 1024 * 1024),
     )(proj_narrow, weight_t, gathered)
 
 

time: 64.9 us -> 68.8 us (1.060)
  Pallas kernels: 58.4 us -> 62.1 us
    pallas_call x1, Pallas kernels: 6.81 us -> 8.89 us  [hidden_gradient(): pl.pallas_call(spread_kernel, grid=(steps,), out_shape=(jax.ShapeDtypeStr...]
    pallas_call x1, Pallas kernels: 51.6 us -> 53.2 us  [exchange(): pl.pallas_call(functools.partial(exchange_kernel, shards, enc_count, doc_...]
    unnamed x5 -> x1, local copies, waits for them, and re-layouts: 2.53 us -> 1.32 us
where the time goes in v4:
time: 68.8 us; the launch traced here: 68.3 us
  Pallas kernels  62.1 us (90%)
  other arithmetic  2.82 us (4%)
  local copies, waits for them, and re-layouts  2.11 us (3%)
  between operations  1.29 us (2%)
    pallas_call x1, Pallas kernels, exchange(): pl.pallas_call(functools.partial(exchange_kernel, shards, enc_count, doc_...  53.2 us
    pallas_call x1, Pallas kernels, hidden_gradient(): pl.pallas_call(spread_kernel, grid=(steps,), out_shape=(jax.ShapeDtypeStr...  8.89 us

profile of v4, /device:TPU:1, one launch (start us, length us, event | category | flops | bytes accessed | tf_op | source)
XLA Modules:
  0.0 68.3 jit_solution(11668003869910376143)
XLA Ops:
  1.3 0.8 %dynamic-slice_convert_fusion = f32[40]{0:T(128)S(1)} fusion(s32[640]{0:T(1024)} %param.15, s32[]{:T(128)S(6)} %select_n.17), kind=kLoop, calls=%fused_computation.8 | loop fusion | flops 40 | bytes 324 | tf_op jit(solution)/shard_map/convert_element_type | solution.py:596
  2.1 0.1 pad.3.clone
  2.1 0.7 %fusion = f32[1,256]{1,0:T(1,128)S(1)} fusion(s32[1,256]{1,0:T(1,128)} %param.13, s32[1,256,1]{1,2,0:T(1,128)} %param.12), kind=kLoop, calls=%fused_computation.7 | loop fusion | flops 768 | bytes 3072 | tf_op jit(solution)/shard_map/convert_element_type | solution.py:592
  2.8 1.3 %maximum_maximum_fusion.list_ref = f32[8,256]{1,0:T(8,128)} fusion(f32[1,256]{1,0:T(1,128)S(1)} %fusion, f32[1,256]{1,0:T(1,128)S(1)} %compare_convert_fusion, f32[1,256]{1,0:T(1,128)} %param.11, f32[8]{0:T(128)S(1)} %pad.3.clone), kind=kLoop, calls=%fused_computation | loop fusion | flops 6144 | bytes 11296 | tf_op jit(solution)/shard_map/concatenate | solution.py:593
  4.2 0.7 %broadcast_in_dim.5.length_ref = f32[40,512]{1,0:T(8,128)} broadcast(f32[40]{0:T(128)S(1)} %dynamic-slice_convert_fusion), dimensions={0} | broadcast | bytes 82080 | tf_op jit(solution)/shard_map/broadcast_in_dim | solution.py:597
  4.9 53.2 %shard_map.103 = (bf16[1280,128]{1,0:T(8,128)(2,1)}, bf16[4096,128]{1,0:T(8,128)(2,1)}, f32[32,128]{1,0:T(8,128)}, bf16[128,4096]{1,0:T(8,128)(2,1)}) custom-call(bf16[1280,4096]{1,0:T(8,128)(2,1)} %bitcast.10, bf16[4096,128]{1,0:T(8,128)(2,1)} %weight_hbm.1, bf16[32,128]{1,0:T(8,128)(2,1)} %bitcast.12, f32[8,256]{1,0:T(8,128)} %maximum_maximum_fusion.list_ref, ...), custom_call_target="tpu_custom_call" | custom-call | tf_op jit(solution)/shard_map/pallas_call | solution.py:512
  58.1 8.9 %shard_map.104 = (bf16[1280,4096]{1,0:T(8,128)(2,1)}, f32[4096,128]{1,0:T(8,128)}) custom-call(bf16[1280,128]{1,0:T(8,128)(2,1)} %get-tuple-element.9.narrow_ref, bf16[128,4096]{1,0:T(8,128)(2,1)} %get-tuple-element.10.weight_t_ref, bf16[4096,128]{1,0:T(8,128)(2,1)} %get-tuple-element.11.gathered_ref), custom_call_target="tpu_custom_call" | custom-call | tf_op jit(solution)/shard_map/pallas_call | solution.py:564
  67.0 1.3 %copy.13 = f32[1,32,128]{2,1,0:T(8,128)} copy(f32[1,32,128]{2,1,0:T(8,128)} %bitcast.11) | data formatting | bytes 32768
  (2 shorter events, 0.0 us)

commit v5 on v4

--- a/solution.py
+++ b/solution.py
@@ -546,7 +546,7 @@
         + [dma((shards,))] * 6
         + [dma((chips,))] * 12,
         compiler_params=pltpu.CompilerParams(
-            collective_id=0, has_side_effects=True, vmem_limit_bytes=60 * 1024 * 1024
+            collective_id=0, has_side_effects=True, vmem_limit_bytes=48 * 1024 * 1024
         ),
     )(flat_hidden, proj_weight, query, lists, lengths)
 
@@ -577,7 +577,7 @@
             pl.BlockSpec((tokens // steps, hid), lambda i: (i, 0)),
             pl.BlockSpec((hid // steps, EMB), lambda i: (i, 0)),
         ),
-        compiler_params=pltpu.CompilerParams(vmem_limit_bytes=60 * 1024 * 1024),
+        compiler_params=pltpu.CompilerParams(vmem_limit_bytes=48 * 1024 * 1024),
     )(proj_narrow, weight_t, gathered)
 
 

time: 68.8 us -> 64.2 us (0.933)
  Pallas kernels: 62.1 us -> 57.7 us
    pallas_call x1, Pallas kernels: 53.2 us -> 50.9 us  [exchange(): pl.pallas_call(functools.partial(exchange_kernel, shards, enc_count, doc_...]
    pallas_call x1, Pallas kernels: 8.89 us -> 6.81 us  [hidden_gradient(): pl.pallas_call(spread_kernel, grid=(steps,), out_shape=(jax.ShapeDtypeStr...]
    unnamed x1 -> x5, local copies, waits for them, and re-layouts: 1.32 us -> 2.53 us
where the time goes in v5:
time: 64.2 us; the launch traced here: 63.9 us
  Pallas kernels  57.7 us (90%)
  local copies, waits for them, and re-layouts  2.68 us (4%)
  other arithmetic  2.22 us (3%)
  between operations  1.3 us (2%)
    pallas_call x1, Pallas kernels, exchange(): pl.pallas_call(functools.partial(exchange_kernel, shards, enc_count, doc_...  50.9 us
    pallas_call x1, Pallas kernels, hidden_gradient(): pl.pallas_call(spread_kernel, grid=(steps,), out_shape=(jax.ShapeDtypeStr...  6.81 us
    unnamed x5, local copies, waits for them, and re-layouts  2.53 us

profile of v5, /device:TPU:1, one launch (start us, length us, event | category | flops | bytes accessed | tf_op | source)
XLA Modules:
  0.0 63.9 jit_solution(9734682895702608759)
XLA Ops:
  1.3 0.8 %dynamic-slice_convert_fusion = f32[40]{0:T(128)S(1)} fusion(s32[640]{0:T(1024)} %param.15, s32[]{:T(128)S(6)} %select_n.17), kind=kLoop, calls=%fused_computation.8 | loop fusion | flops 40 | bytes 324 | tf_op jit(solution)/shard_map/convert_element_type | solution.py:596
  2.1 0.1 pad.3.clone
  2.1 0.7 %fusion = f32[1,256]{1,0:T(1,128)S(1)} fusion(s32[1,256]{1,0:T(1,128)} %param.13, s32[1,256,1]{1,2,0:T(1,128)} %param.12), kind=kLoop, calls=%fused_computation.7 | loop fusion | flops 768 | bytes 3072 | tf_op jit(solution)/shard_map/convert_element_type | solution.py:592
  2.8 0.7 %maximum_maximum_fusion.list_ref = f32[8,256]{1,0:T(8,128)S(1)} fusion(f32[1,256]{1,0:T(1,128)S(1)} %fusion, f32[1,256]{1,0:T(1,128)S(1)} %compare_convert_fusion, f32[1,256]{1,0:T(1,128)} %param.11, f32[8]{0:T(128)S(1)} %pad.3.clone), kind=kLoop, calls=%fused_computation | loop fusion | flops 6144 | bytes 11296 | tf_op jit(solution)/shard_map/concatenate | solution.py:593
  3.6 0.1 broadcast_in_dim.5.length_ref
  3.7 0.0 copy-start
  3.7 1.2 %copy-done = bf16[4096,128]{1,0:T(8,128)(2,1)S(1)} copy-done((bf16[4096,128]{1,0:T(8,128)(2,1)S(1)}, bf16[4096,128]{1,0:T(8,128)(2,1)}, u32[]{:S(2)}) %copy-start) | copy-done | bytes 1048600
  4.9 0.0 copy-start.1
  4.9 0.7 %copy-done.1 = bf16[1,32,128]{2,1,0:T(8,128)(2,1)S(1)} copy-done((bf16[1,32,128]{2,1,0:T(8,128)(2,1)S(1)}, bf16[1,32,128]{2,1,0:T(8,128)(2,1)}, u32[]{:S(2)}) %copy-start.1) | copy-done | bytes 8216
  5.6 50.9 %shard_map.103 = (bf16[1280,128]{1,0:T(8,128)(2,1)S(1)}, bf16[4096,128]{1,0:T(8,128)(2,1)S(1)}, f32[32,128]{1,0:T(8,128)S(1)}, bf16[128,4096]{1,0:T(8,128)(2,1)S(1)}) custom-call(bf16[1280,4096]{1,0:T(8,128)(2,1)} %bitcast.12, bf16[4096,128]{1,0:T(8,128)(2,1)S(1)} %copy-done, bf16[32,128]{1,0:T(8,128)(2,1)S(1)} %bitcast.11, ...), custom_call_target="tpu_custom_call" | custom-call | tf_op jit(solution)/shard_map/pallas_call | solution.py:512
  56.5 6.8 %shard_map.104 = (bf16[1280,4096]{1,0:T(8,128)(2,1)}, f32[4096,128]{1,0:T(8,128)}) custom-call(bf16[1280,128]{1,0:T(8,128)(2,1)S(1)} %get-tuple-element.9.narrow_ref, bf16[128,4096]{1,0:T(8,128)(2,1)S(1)} %get-tuple-element.10.weight_t_ref, bf16[4096,128]{1,0:T(8,128)(2,1)S(1)} %get-tuple-element.11.gathered_ref), custom_call_target="tpu_custom_call" | custom-call | tf_op jit(solution)/shard_map/pallas_call | solution.py:564
  63.3 0.6 copy.13
  (2 shorter events, 0.0 us)
Async XLA Ops:
  3.7 1.2 %copy-start = (bf16[4096,128]{1,0:T(8,128)(2,1)S(1)}, bf16[4096,128]{1,0:T(8,128)(2,1)}, u32[]{:S(2)}) copy-start(bf16[4096,128]{1,0:T(8,128)(2,1)} %weight_hbm.1) | copy-start | bytes 3145732
  4.9 0.7 %copy-start.1 = (bf16[1,32,128]{2,1,0:T(8,128)(2,1)S(1)}, bf16[1,32,128]{2,1,0:T(8,128)(2,1)}, u32[]{:S(2)}) copy-start(bf16[1,32,128]{2,1,0:T(8,128)(2,1)} %param.10) | copy-start | bytes 24580
